TPU v7x, 128 devices: a whole 4x4x4 slice. The times are simulated.
128 devices in a mesh: macro: 4 (over y), rve: 32 (over z, x, core).
Axes of the slice: x: 4, y: 4, z: 4, core: 2. Of those that a mesh axis runs over, the one named last changes fastest.
Arguments:
- displacement: float32 [3, 128, 8, 16], P(None, ('macro', 'rve')), may hold values from -1.5 to 1.5
- velocity: float32 [3, 128, 8, 16], P(None, ('macro', 'rve')), may hold values from -3 to 3
- old_owner: int32 [16384, 1], P(('macro', 'rve')), may hold values from 0 to 31; in each aligned block of 128 rows (0 to 127, 128 to 255, ...) at most 8 rows name the same one
- new_owner: int32 [16384, 1], P(('macro', 'rve')), may hold values from 0 to 31; in each aligned block of 128 rows (0 to 127, 128 to 255, ...) at most 8 rows name the same one
- substeps: int32 [16384], P(('macro', 'rve')), may hold values from 1 to 8
- strut_ends: int32 [2, 4096], replicated, may hold values from 0 to 511, as said below
- flow_stress: float32 [4096], replicated, may hold values from 0.2 to 2
- relax_rate: float32 [4096], replicated, may hold values from 0.02 to 0.3
- plastic_old: float32 [32768, 4096], P(('macro', 'rve')), may hold values from -0.5 to 0.5
Outputs:
- displacement_next: float32 [3, 128, 8, 16], P(None, ('macro', 'rve'))
- velocity_next: float32 [3, 128, 8, 16], P(None, ('macro', 'rve'))
- plastic_new: float32 [32768, 4096], P(('macro', 'rve'))
Inputs may be any that keep to these rules, and one draw needn't show every extreme that they name: `old_owner`: the elements of one device name one owner at most 8 times, a bound that some block reaches. `new_owner`: the elements of one device name one owner at most 8 times, a bound that some block reaches. `strut_ends`: the two nodes of a strut are distinct and their lattice coordinates differ by at most one along each dimension, modulo 8.
All inputs are finite; a program needn't handle non-finite values.
Results may differ from a plain program's by a relative error of at most 0.0003.
Values sent between devices are 32-bit elements; how exact they have to be, the bound alone decides.
No kernel may reach another device: no remote copies, remote signals or barrier semaphores. Data moves between devices by JAX's collectives and lax.ppermute only.
A program may use at most 64 MiB of HBM per device.

v0:
```python
import jax
import jax.numpy as jnp
from jax import lax
from jax.sharding import PartitionSpec as P

STRUTS = 4096
NSUB = 8
LATTICE = 8


young = 10.0
harden = 1.0
time_step = 0.2
highest = lax.Precision.HIGHEST


def from_behind(value, axis, steps):
    count = lax.axis_size(axis)
    initial, last = (max(0, -steps), min(count, count - steps))
    return lax.ppermute(value, axis, [(source, source + steps) for source in range(initial, last)])


def lattice_coords(node_ids):
    lattice_side = LATTICE
    return jnp.stack(
        [
            node_ids // (lattice_side * lattice_side),
            node_ids // lattice_side % lattice_side,
            node_ids % lattice_side,
        ]
    )


def strut_basis(strut_ends):
    offset = lattice_coords(strut_ends[1]) - lattice_coords(strut_ends[0])
    offset = (offset + LATTICE // 2) % LATTICE - LATTICE // 2
    vector = offset.astype(jnp.float32)
    length = jnp.sqrt(jnp.sum(vector * vector, axis=0))
    direction = vector / length
    dir_x, dir_y, dir_z = (direction[0], direction[1], direction[2])
    strain_basis = jnp.stack(
        [
            dir_x * dir_x,
            dir_y * dir_y,
            dir_z * dir_z,
            2.0 * dir_x * dir_y,
            2.0 * dir_x * dir_z,
            2.0 * dir_y * dir_z,
        ]
    )
    stress_basis = (
        jnp.stack(
            [
                dir_x * dir_x,
                dir_y * dir_y,
                dir_z * dir_z,
                dir_x * dir_y,
                dir_x * dir_z,
                dir_y * dir_z,
            ]
        )
        / STRUTS
    )
    return (strain_basis, stress_basis)


def green(deform):

    def column_dot(col_a, col_b):
        return (
            deform[col_a] * deform[col_b]
            + deform[3 + col_a] * deform[3 + col_b]
            + deform[6 + col_a] * deform[6 + col_b]
        )

    return 0.5 * jnp.stack(
        [
            column_dot(0, 0) - 1.0,
            column_dot(1, 1) - 1.0,
            column_dot(2, 2) - 1.0,
            column_dot(0, 1),
            column_dot(0, 2),
            column_dot(1, 2),
        ]
    )


def relax(deform_old, deform_new, counts, plastic, flow_stress, relax_rate, strain_basis):
    step_count = jnp.maximum(counts, 1.0)
    change = deform_new - deform_old
    rate_step = relax_rate[None, :] / step_count[:, None]
    factor = rate_step / (1.0 + (young + harden) * rate_step)

    def advance(turn_index, plastic):
        turn_level = (turn_index + 1).astype(counts.dtype)
        deform = deform_old + (turn_level / step_count)[None, :] * change
        strain = jnp.einsum("cr,cs->rs", green(deform), strain_basis, precision=highest)
        trial_stress = young * (strain - plastic) - harden * plastic
        excess = jnp.maximum(jnp.abs(trial_stress) - flow_stress[None, :], 0.0)
        active_mask = (turn_level <= counts)[:, None]
        return plastic + jnp.where(active_mask, excess * factor * jnp.sign(trial_stress), 0.0)

    return lax.fori_loop(0, NSUB, advance, plastic)


def homogenize(deform_new, plastic, strain_basis, stress_basis):
    strain = jnp.einsum("cr,cs->rs", green(deform_new), strain_basis, precision=highest)
    strut_stress = young * (strain - plastic)
    return jnp.einsum("rs,cs->cr", strut_stress, stress_basis, precision=highest)


def first_stress(deform, stress):
    pairing = ((0, 3, 4), (3, 1, 5), (4, 5, 2))
    components = []
    for row_axis in range(3):
        for col_axis in range(3):
            components.append(
                deform[3 * row_axis] * stress[pairing[0][col_axis]]
                + deform[3 * row_axis + 1] * stress[pairing[1][col_axis]]
                + deform[3 * row_axis + 2] * stress[pairing[2][col_axis]]
            )
    return jnp.stack(components)


def element_deform(extended):
    plane_low = extended[:, :-1]
    plane_high = extended[:, 1:]

    def roll_second(values):
        return jnp.roll(values, -1, axis=2)

    def roll_third(values):
        return jnp.roll(values, -1, axis=3)

    diff_first = plane_high - plane_low
    slope_first = 0.25 * (
        diff_first
        + roll_second(diff_first)
        + roll_third(diff_first)
        + roll_second(roll_third(diff_first))
    )
    plane_mid = 0.5 * (plane_low + plane_high)
    diff_second = roll_second(plane_mid) - plane_mid
    slope_second = 0.5 * (diff_second + roll_third(diff_second))
    diff_third = roll_third(plane_mid) - plane_mid
    slope_third = 0.5 * (diff_third + roll_second(diff_third))
    slopes = jnp.stack([slope_first, slope_second, slope_third], axis=1)
    identity = jnp.eye(3, dtype=extended.dtype)
    slopes = slopes + identity[:, :, None, None, None]
    return slopes.reshape(9, -1)


def nodal_force(piola, layout):
    tensor = piola.reshape((3, 3) + layout)
    planes = layout[0]
    nodal = jnp.zeros((3, planes + 1, layout[1], layout[2]), piola.dtype)
    for offset_plane in (0, 1):
        for offset_row in (0, 1):
            for offset_col in (0, 1):
                corner_term = 0.25 * (
                    (2 * offset_plane - 1) * tensor[:, 0]
                    + (2 * offset_row - 1) * tensor[:, 1]
                    + (2 * offset_col - 1) * tensor[:, 2]
                )
                corner_term = jnp.roll(
                    jnp.roll(corner_term, offset_row, axis=2), offset_col, axis=3
                )
                nodal = nodal.at[:, offset_plane : offset_plane + planes].add(corner_term)
    return nodal


def ranks(owner_map, owner_count):
    one_hot = (owner_map[:, :, None] == jnp.arange(owner_count, dtype=jnp.int32)).astype(jnp.int32)
    earlier = jnp.cumsum(one_hot, axis=1) - one_hot
    return jnp.sum(earlier * one_hot, axis=2)


def shards(
    displacement,
    velocity,
    old_owner,
    new_owner,
    substeps,
    strut_ends,
    flow_stress,
    relax_rate,
    plastic_old,
):
    strain_basis, stress_basis = strut_basis(strut_ends)
    owners = lax.axis_size("rve")
    capacity = plastic_old.shape[0] // owners
    planes = displacement.shape[1]
    displacement_next = displacement + time_step * velocity
    rim_now, rim_next = from_behind((displacement, displacement_next), ("macro", "rve"), -1)
    deform_old = element_deform(jnp.concatenate([displacement, rim_now], axis=1))
    deform_new = element_deform(jnp.concatenate([displacement_next, rim_next], axis=1))
    old_map = old_owner.reshape(1, -1)
    new_map = new_owner.reshape(1, -1)
    old_slots = (old_map * capacity + ranks(old_map, owners)).reshape(-1)
    new_slots = (new_map * capacity + ranks(new_map, owners)).reshape(-1)
    counts = substeps.astype(jnp.float32)
    packed = jnp.concatenate([deform_old, deform_new, counts[None, :]], axis=0)
    outgoing = jnp.zeros((19, owners * capacity), jnp.float32).at[:, old_slots].set(packed)
    incoming = lax.all_to_all(outgoing, "rve", split_axis=1, concat_axis=1, tiled=True)
    updated = relax(
        incoming[:9],
        incoming[9:18],
        incoming[18],
        plastic_old,
        flow_stress,
        relax_rate,
        strain_basis,
    )
    returned = lax.all_to_all(updated, "rve", split_axis=0, concat_axis=0, tiled=True)
    plastic = returned[old_slots]
    stress = homogenize(deform_new, plastic, strain_basis, stress_basis)
    piola = first_stress(deform_new, stress)
    nodal = nodal_force(piola, (planes, displacement.shape[2], displacement.shape[3]))
    carried = from_behind(nodal[:, planes:], ("macro", "rve"), 1)
    interior = nodal[:, :planes].at[:, :1].add(carried)
    velocity_next = velocity - time_step * interior
    moving = jnp.zeros_like(plastic_old).at[new_slots].set(plastic)
    plastic_new = lax.all_to_all(moving, "rve", split_axis=0, concat_axis=0, tiled=True)
    return (displacement_next, velocity_next, plastic_new)


def solution(mesh):
    in_specs = (
        P(None, ("macro", "rve"), None, None),
        P(None, ("macro", "rve"), None, None),
        P(("macro", "rve"), None),
        P(("macro", "rve"), None),
        P(("macro", "rve")),
        P(),
        P(),
        P(),
        P(("macro", "rve"), None),
    )
    out_specs = (
        P(None, ("macro", "rve"), None, None),
        P(None, ("macro", "rve"), None, None),
        P(("macro", "rve"), None),
    )
    return jax.shard_map(shards, mesh=mesh, in_specs=in_specs, out_specs=out_specs, check_vma=False)
```

profile of v0, /device:TPU:24, one launch (start us, length us, event | category | flops | bytes accessed | tf_op | source)
XLA Modules:
  0.0 242.6 jit_solution(15974991268300332162)
XLA Ops:
  0.7 4.7 %copy.84 = f32[256,4096]{1,0:T(8,128)} copy(f32[256,4096]{1,0:T(8,128)} %param.39) | data formatting | bytes 8388608
  5.4 7.9 %collective-permute-start.1 = (f32[3,1,8,16]{3,2,0,1:T(8,128)S(1)}, f32[3,1,8,16]{3,2,0,1:T(8,128)S(1)}, u32[]{:S(2)}, u32[]{:S(2)}) collective-permute-start(f32[3,1,8,16]{3,2,0,1:T(8,128)S(1)} %bitcast.197), channel_id=1, source_target_pairs={{1,0},{2,1},{3,2},{4,3},{5,4},{6,5},{7,6},{8,7},{9,8},{10,9},{11,1... | collective-permute-start | bytes 4616 | tf_op jit(solution)/shard_map/ppermute | solution.py:20
  13.3 2.6 %collective-permute-start = (f32[3,1,8,16]{3,2,0,1:T(8,128)S(1)}, f32[3,1,8,16]{3,2,0,1:T(8,128)S(1)}, u32[]{:S(2)}, u32[]{:S(2)}) collective-permute-start(f32[3,1,8,16]{3,2,0,1:T(8,128)S(1)} %bitcast.194), channel_id=1, source_target_pairs={{1,0},{2,1},{3,2},{4,3},{5,4},{6,5},{7,6},{8,7},{9,8},{10,9},{11,1... | collective-permute-start | bytes 4616 | tf_op jit(solution)/shard_map/ppermute | solution.py:20
  16.0 0.2 reduce_window_sum.17
  16.2 0.2 select_reduce_fusion.1
  16.4 0.4 and_select_fusion.5
  16.8 0.2 multiply_reduce_fusion
  17.1 0.1 reshape.919
  18.5 0.1 fusion.40
  18.8 0.1 copy.64
  18.9 0.9 scatter_custom_fusion
  19.8 0.8 reshape.949
  20.6 4.8 %all-to-all-start = ((f32[32,1,152]{2,1,0:T(1,128)}), f32[32,1,152]{2,1,0:T(1,128)S(1)}, u32[]{:S(2)}, u32[]{:S(2)}) async-start(f32[32,1,152]{2,1,0:T(1,128)} %reshape.949), calls=%async_computation | async-start | bytes 65536 | tf_op jit(solution)/shard_map/all_to_all | solution.py:204
  25.4 0.1 slice_multiply_fusion
  25.5 0.2 stack.117
  25.6 7.2 %all-to-all-done = f32[32,1,152]{2,1,0:T(1,128)S(1)} async-done(((f32[32,1,152]{2,1,0:T(1,128)}), f32[32,1,152]{2,1,0:T(1,128)S(1)}, u32[]{:S(2)}, u32[]{:S(2)}) %all-to-all-start) | async-done | bytes 19488 | tf_op jit(solution)/shard_map/all_to_all | solution.py:204
  32.8 0.5 broadcast.760
  33.3 0.7 reduce.22
  34.1 0.1 reshape.950
  34.2 0.2 slice_reduce_fusion
  34.4 0.1 slice_bitcast_fusion
  34.4 0.1 squeeze.26
  34.6 0.1 copy.72
  34.8 78.0 %while.28 = (s32[]{:T(128)}, f32[256,4096]{1,0:T(8,128)}, f32[256]{0:T(256)S(1)}, f32[256]{0:T(256)S(1)}, f32[9,256]{1,0:T(8,128)S(1)}, /*index=5*/f32[9,256]{1,...) while((s32[]{:T(128)}, f32[256,4096]{1,0:T(8,128)}, ...), condition=%wide.region_5.6_spmd.clone.clone, body=%wide.region_4.5_spmd.clone.clone.sunk | while | flops 92289792 | bytes 8593013 | solution.py:103
  34.9 9.6 %select_add_fusion.2 = f32[256,4096]{1,0:T(8,128)} fusion(f32[256,4096]{1,0:T(8,128)} %get-tuple-element.568, f32[6,4096]{1,0:T(8,128)S(1)} %get-tuple-element.583, f32[256]{0:T(256)S(1)} %get-tuple-element.580, f32[4096]{0:T(1024)S(1)} %get-tuple-element.585, f32[4096]{0:T(1024)S(1)} %get-tuple-element.584, ...), kind=kOutput, calls=%fused_computation.13.clone.1 | convolution fusion | flops 92276224 | bytes 8527104 | tf_op jit(solution)/shard_map/while/body/eval_jaxpr/cr,cs->rs/dot_general | solution.py:97
  44.6 9.6 %select_add_fusion.2 = f32[256,4096]{1,0:T(8,128)} fusion(f32[256,4096]{1,0:T(8,128)} %get-tuple-element.568, f32[6,4096]{1,0:T(8,128)S(1)} %get-tuple-element.583, f32[256]{0:T(256)S(1)} %get-tuple-element.580, f32[4096]{0:T(1024)S(1)} %get-tuple-element.585, f32[4096]{0:T(1024)S(1)} %get-tuple-element.584, ...), kind=kOutput, calls=%fused_computation.13.clone.1 | convolution fusion | flops 92276224 | bytes 8527104 | tf_op jit(solution)/shard_map/while/body/eval_jaxpr/cr,cs->rs/dot_general | solution.py:97
  54.4 9.6 %select_add_fusion.2 = f32[256,4096]{1,0:T(8,128)} fusion(f32[256,4096]{1,0:T(8,128)} %get-tuple-element.568, f32[6,4096]{1,0:T(8,128)S(1)} %get-tuple-element.583, f32[256]{0:T(256)S(1)} %get-tuple-element.580, f32[4096]{0:T(1024)S(1)} %get-tuple-element.585, f32[4096]{0:T(1024)S(1)} %get-tuple-element.584, ...), kind=kOutput, calls=%fused_computation.13.clone.1 | convolution fusion | flops 92276224 | bytes 8527104 | tf_op jit(solution)/shard_map/while/body/eval_jaxpr/cr,cs->rs/dot_general | solution.py:97
  64.1 9.6 %select_add_fusion.2 = f32[256,4096]{1,0:T(8,128)} fusion(f32[256,4096]{1,0:T(8,128)} %get-tuple-element.568, f32[6,4096]{1,0:T(8,128)S(1)} %get-tuple-element.583, f32[256]{0:T(256)S(1)} %get-tuple-element.580, f32[4096]{0:T(1024)S(1)} %get-tuple-element.585, f32[4096]{0:T(1024)S(1)} %get-tuple-element.584, ...), kind=kOutput, calls=%fused_computation.13.clone.1 | convolution fusion | flops 92276224 | bytes 8527104 | tf_op jit(solution)/shard_map/while/body/eval_jaxpr/cr,cs->rs/dot_general | solution.py:97
  73.9 9.6 %select_add_fusion.2 = f32[256,4096]{1,0:T(8,128)} fusion(f32[256,4096]{1,0:T(8,128)} %get-tuple-element.568, f32[6,4096]{1,0:T(8,128)S(1)} %get-tuple-element.583, f32[256]{0:T(256)S(1)} %get-tuple-element.580, f32[4096]{0:T(1024)S(1)} %get-tuple-element.585, f32[4096]{0:T(1024)S(1)} %get-tuple-element.584, ...), kind=kOutput, calls=%fused_computation.13.clone.1 | convolution fusion | flops 92276224 | bytes 8527104 | tf_op jit(solution)/shard_map/while/body/eval_jaxpr/cr,cs->rs/dot_general | solution.py:97
  83.6 9.6 %select_add_fusion.2 = f32[256,4096]{1,0:T(8,128)} fusion(f32[256,4096]{1,0:T(8,128)} %get-tuple-element.568, f32[6,4096]{1,0:T(8,128)S(1)} %get-tuple-element.583, f32[256]{0:T(256)S(1)} %get-tuple-element.580, f32[4096]{0:T(1024)S(1)} %get-tuple-element.585, f32[4096]{0:T(1024)S(1)} %get-tuple-element.584, ...), kind=kOutput, calls=%fused_computation.13.clone.1 | convolution fusion | flops 92276224 | bytes 8527104 | tf_op jit(solution)/shard_map/while/body/eval_jaxpr/cr,cs->rs/dot_general | solution.py:97
  93.3 9.6 %select_add_fusion.2 = f32[256,4096]{1,0:T(8,128)} fusion(f32[256,4096]{1,0:T(8,128)} %get-tuple-element.568, f32[6,4096]{1,0:T(8,128)S(1)} %get-tuple-element.583, f32[256]{0:T(256)S(1)} %get-tuple-element.580, f32[4096]{0:T(1024)S(1)} %get-tuple-element.585, f32[4096]{0:T(1024)S(1)} %get-tuple-element.584, ...), kind=kOutput, calls=%fused_computation.13.clone.1 | convolution fusion | flops 92276224 | bytes 8527104 | tf_op jit(solution)/shard_map/while/body/eval_jaxpr/cr,cs->rs/dot_general | solution.py:97
  103.1 9.6 %select_add_fusion.2 = f32[256,4096]{1,0:T(8,128)} fusion(f32[256,4096]{1,0:T(8,128)} %get-tuple-element.568, f32[6,4096]{1,0:T(8,128)S(1)} %get-tuple-element.583, f32[256]{0:T(256)S(1)} %get-tuple-element.580, f32[4096]{0:T(1024)S(1)} %get-tuple-element.585, f32[4096]{0:T(1024)S(1)} %get-tuple-element.584, ...), kind=kOutput, calls=%fused_computation.13.clone.1 | convolution fusion | flops 92276224 | bytes 8527104 | tf_op jit(solution)/shard_map/while/body/eval_jaxpr/cr,cs->rs/dot_general | solution.py:97
  112.7 5.0 %all-to-all-start.1 = ((f32[32,8,4096]{2,1,0:T(8,128)}), f32[32,8,4096]{2,1,0:T(8,128)}, u32[]{:S(2)}, u32[]{:S(2)}) async-start(f32[32,8,4096]{2,1,0:T(8,128)} %bitcast.172), calls=%async_computation.1 | async-start | bytes 8388608 | tf_op jit(solution)/shard_map/all_to_all | solution.py:214
  117.8 0.2 reduce_window_sum.18
  118.0 0.2 select_reduce_fusion
  118.2 53.0 %all-to-all-done.1 = f32[32,8,4096]{2,1,0:T(8,128)} async-done(((f32[32,8,4096]{2,1,0:T(8,128)}), f32[32,8,4096]{2,1,0:T(8,128)}, u32[]{:S(2)}, u32[]{:S(2)}) %all-to-all-start.1) | async-done | bytes 4194336 | tf_op jit(solution)/shard_map/all_to_all | solution.py:214
  171.2 4.4 %gather_fusion = f32[128,4096]{1,0:T(8,128)S(1)} fusion(f32[256,4096]{1,0:T(8,128)} %bitcast.26, s32[1024]{0:T(1024)S(1)} %pad_clamp_fusion), kind=kCustom, calls=%fused_computation | custom fusion | bytes 4194816 | tf_op jit(solution)/shard_map/gather | solution.py:215
  175.6 4.0 %scatter_custom_fusion.1 = f32[256,4096]{1,0:T(8,128)} fusion(s32[128]{0:T(128)S(1)} %fusion.60, f32[128,4096]{1,0:T(8,128)S(1)} %gather_fusion, f32[]{:T(128)} %constant.380.clone.1), kind=kCustom, calls=%fused_computation.28 | custom fusion | bytes 4194308 | tf_op jit(solution)/shard_map/scatter | solution.py:222
  179.6 5.0 %all-to-all-start.2 = ((f32[32,8,4096]{2,1,0:T(8,128)}), f32[32,8,4096]{2,1,0:T(8,128)}, u32[]{:S(2)}, u32[]{:S(2)}) async-start(f32[32,8,4096]{2,1,0:T(8,128)} %bitcast.173), calls=%async_computation.2 | async-start | bytes 8388608 | tf_op jit(solution)/shard_map/all_to_all | solution.py:223
  184.7 0.2 stack.115
  184.9 1.9 fusion.12
  186.8 1.7 fusion.15
  188.9 0.1 fusion.30
  189.0 1.9 collective-permute-start.2
  191.1 44.2 %collective-permute-done.2 = f32[3,1,8,16]{3,2,0,1:T(8,128)S(1)} collective-permute-done((f32[3,1,8,16]{3,2,0,1:T(8,128)S(1)}, f32[3,1,8,16]{3,2,0,1:T(8,128)S(1)}, u32[]{:S(2)}, u32[]{:S(2)}) %collective-permute-start.2) | collective-permute-done | bytes 1568 | tf_op jit(solution)/shard_map/ppermute | solution.py:20
  235.3 0.7 fusion.36
  236.0 2.0 all-to-all-done.2
  238.0 4.7 %copy.85 = f32[256,4096]{1,0:T(8,128)} copy(f32[256,4096]{1,0:T(8,128)} %bitcast.35) | data formatting | bytes 8388608
  (139 shorter events, 2.9 us)
Async XLA Ops:
  0.6 4.7 %copy-start.2 = (f32[3,1,8,16]{3,2,1,0:T(8,128)S(1)}, f32[3,1,8,16]{3,2,1,0:T(8,128)}, u32[]{:S(2)}) copy-start(f32[3,1,8,16]{3,2,1,0:T(8,128)} %param.31) | copy-start | bytes 4612
  0.6 12.6 %copy-start.1 = (f32[3,1,8,16]{3,2,1,0:T(8,128)S(1)}, f32[3,1,8,16]{3,2,1,0:T(8,128)}, u32[]{:S(2)}) copy-start(f32[3,1,8,16]{3,2,1,0:T(8,128)} %param.32) | copy-start | bytes 4612
  0.7 15.2 %copy-start.4 = (s32[128,1]{0,1:T(1,128)S(1)}, s32[128,1]{0,1:T(1,128)}, u32[]{:S(2)}) copy-start(s32[128,1]{0,1:T(1,128)} %param.33) | copy-start | bytes 1540
  0.7 15.7 %copy-start.8 = (s32[128]{0:T(128)S(1)}, s32[128]{0:T(128)}, u32[]{:S(2)}) copy-start(s32[128]{0:T(128)} %param.35) | copy-start | bytes 1540
  0.7 15.7 %copy-start.3 = (s32[2,4096]{1,0:T(2,128)S(1)}, s32[2,4096]{1,0:T(2,128)}, u32[]{:S(2)}) copy-start(s32[2,4096]{1,0:T(2,128)} %param.36) | copy-start | bytes 98308
  5.4 29.4 %copy-start.6 = (f32[4096]{0:T(1024)S(1)}, f32[4096]{0:T(1024)}, u32[]{:S(2)}) copy-start(f32[4096]{0:T(1024)} %param.37) | copy-start | bytes 49156
  5.4 29.4 %copy-start.7 = (f32[4096]{0:T(1024)S(1)}, f32[4096]{0:T(1024)}, u32[]{:S(2)}) copy-start(f32[4096]{0:T(1024)} %param.38) | copy-start | bytes 49156
  5.4 11.8 %collective-permute-start.1 = (f32[3,1,8,16]{3,2,0,1:T(8,128)S(1)}, f32[3,1,8,16]{3,2,0,1:T(8,128)S(1)}, u32[]{:S(2)}, u32[]{:S(2)}) collective-permute-start(f32[3,1,8,16]{3,2,0,1:T(8,128)S(1)} %bitcast.197), channel_id=1, source_target_pairs={{1,0},{2,1},{3,2},{4,3},{5,4},{6,5},{7,6},{8,7},{9,8},{10,9},{11,1... | collective-permute-start | bytes 4616 | tf_op jit(solution)/shard_map/ppermute | solution.py:20
  13.3 21.5 %copy-start = (f32[3,1,8,16]{3,2,1,0:T(8,128)}, f32[3,1,8,16]{3,2,1,0:T(8,128)S(1)}, u32[]{:S(2)}) copy-start(f32[3,1,8,16]{3,2,1,0:T(8,128)S(1)} %multiply_add_fusion.4) | copy-start | bytes 4612
  13.3 4.3 %collective-permute-start = (f32[3,1,8,16]{3,2,0,1:T(8,128)S(1)}, f32[3,1,8,16]{3,2,0,1:T(8,128)S(1)}, u32[]{:S(2)}, u32[]{:S(2)}) collective-permute-start(f32[3,1,8,16]{3,2,0,1:T(8,128)S(1)} %bitcast.194), channel_id=1, source_target_pairs={{1,0},{2,1},{3,2},{4,3},{5,4},{6,5},{7,6},{8,7},{9,8},{10,9},{11,1... | collective-permute-start | bytes 4616 | tf_op jit(solution)/shard_map/ppermute | solution.py:20
  20.6 12.2 %all-to-all-start = ((f32[32,1,152]{2,1,0:T(1,128)}), f32[32,1,152]{2,1,0:T(1,128)S(1)}, u32[]{:S(2)}, u32[]{:S(2)}) async-start(f32[32,1,152]{2,1,0:T(1,128)} %reshape.949), calls=%async_computation | async-start | bytes 65536 | tf_op jit(solution)/shard_map/all_to_all | solution.py:204
  112.7 5.0 %copy-start.5 = (s32[128,1]{0,1:T(1,128)S(1)}, s32[128,1]{0,1:T(1,128)}, u32[]{:S(2)}) copy-start(s32[128,1]{0,1:T(1,128)} %param.34) | copy-start | bytes 1540
  112.7 58.5 %all-to-all-start.1 = ((f32[32,8,4096]{2,1,0:T(8,128)}), f32[32,8,4096]{2,1,0:T(8,128)}, u32[]{:S(2)}, u32[]{:S(2)}) async-start(f32[32,8,4096]{2,1,0:T(8,128)} %bitcast.172), calls=%async_computation.1 | async-start | bytes 8388608 | tf_op jit(solution)/shard_map/all_to_all | solution.py:214
  179.6 58.3 %all-to-all-start.2 = ((f32[32,8,4096]{2,1,0:T(8,128)}), f32[32,8,4096]{2,1,0:T(8,128)}, u32[]{:S(2)}, u32[]{:S(2)}) async-start(f32[32,8,4096]{2,1,0:T(8,128)} %bitcast.173), calls=%async_computation.2 | async-start | bytes 8388608 | tf_op jit(solution)/shard_map/all_to_all | solution.py:223
  189.0 46.3 %collective-permute-start.2 = (f32[3,1,8,16]{3,2,0,1:T(8,128)S(1)}, f32[3,1,8,16]{3,2,0,1:T(8,128)S(1)}, u32[]{:S(2)}, u32[]{:S(2)}) collective-permute-start(f32[3,1,8,16]{3,2,0,1:T(8,128)S(1)} %fusion.30), channel_id=1, source_target_pairs={{0,1},{1,2},{2,3},{3,4},{4,5},{5,6},{6,7},{7,8},{8,9},{9,10},{10,1... | collective-permute-start | bytes 4616 | tf_op jit(solution)/shard_map/ppermute | solution.py:20
where the time goes:
time: 245 us; the launch traced here: 243 us
  waiting for transfers between devices  106 us (43%)
  matrix products  80.8 us (33%)
  starting transfers between devices  27.2 us (11%)
  local copies, waits for them, and re-layouts  22.3 us (9%)
  other arithmetic  4.52 us (2%)
    dot_general x8, matrix products, advance(): jnp.einsum('cr,cs->rs', green(deform), strain_basis, precision=highest)  77.2 us
    all_to_all x1, waiting for transfers between devices, shards(): lax.all_to_all(updated, 'rve', split_axis=0, concat_axis=0, tiled=True)  53 us
    ppermute x3, waiting for transfers between devices, from_behind(): lax.ppermute(value, axis, [(source, source + steps) for source in range(i...  44.2 us
    ppermute x3, starting transfers between devices, from_behind(): lax.ppermute(value, axis, [(source, source + steps) for source in range(i...  12.4 us
    unnamed x23, local copies, waits for them, and re-layouts  10.2 us
    all_to_all x1, waiting for transfers between devices, shards(): lax.all_to_all(outgoing, 'rve', split_axis=1, concat_axis=1, tiled=True)  7.16 us
    all_to_all x1, starting transfers between devices, shards(): lax.all_to_all(moving, 'rve', split_axis=0, concat_axis=0, tiled=True)  5.04 us
    all_to_all x1, starting transfers between devices, shards(): lax.all_to_all(updated, 'rve', split_axis=0, concat_axis=0, tiled=True)  5 us
  transfers between devices with their start and end apart: 6, of which 4 were waited for; matrix products, arithmetic and copies ran while one was open for 3% of the time, Pallas kernels for 0%

commit v1 on v0

v1 whole, which is shorter than its diff:
```python
import functools

import jax
import jax.numpy as jnp
import numpy as np
from jax import lax
from jax.experimental import pallas as pl
from jax.experimental.pallas import tpu as pltpu
from jax.sharding import PartitionSpec as P

STRUTS = 4096
NSUB = 8
LATTICE = 8
LANES = 128
POINTS = 128
TILES = STRUTS // LANES
QUADS = TILES // 8

young = 10.0
harden = 1.0
time_step = 0.2
highest = lax.Precision.HIGHEST


def from_behind(value, axis, steps):
    count = lax.axis_size(axis)
    initial, last = (max(0, -steps), min(count, count - steps))
    return lax.ppermute(value, axis, [(source, source + steps) for source in range(initial, last)])


def direction_products():
    table = np.zeros((6, LANES), np.float32)
    for code in range(27):
        vector = np.array([code // 9 - 1, code // 3 % 3 - 1, code % 3 - 1], np.float32)
        length = np.sqrt(np.sum(vector * vector, dtype=np.float32))
        if length == 0:
            continue
        x, y, z = vector / length
        table[:, code] = [x * x, y * y, z * z, x * y, x * z, y * z]
    return table


def direction_codes(strut_ends):
    first, second = strut_ends[0], strut_ends[1]

    def step(scale):
        offset = second // scale % LATTICE - first // scale % LATTICE
        return (offset + LATTICE // 2) % LATTICE - LATTICE // 2

    code = (step(LATTICE * LATTICE) + 1) * 9 + (step(LATTICE) + 1) * 3 + (step(1) + 1)
    return code.reshape(TILES, LANES)


def green(deform):

    def column_dot(col_a, col_b):
        return (
            deform[col_a] * deform[col_b]
            + deform[3 + col_a] * deform[3 + col_b]
            + deform[6 + col_a] * deform[6 + col_b]
        )

    return 0.5 * jnp.stack(
        [
            column_dot(0, 0) - 1.0,
            column_dot(1, 1) - 1.0,
            column_dot(2, 2) - 1.0,
            column_dot(0, 1),
            column_dot(0, 2),
            column_dot(1, 2),
        ]
    )


def first_stress(deform, stress):
    pairing = ((0, 3, 4), (3, 1, 5), (4, 5, 2))
    components = []
    for row_axis in range(3):
        for col_axis in range(3):
            components.append(
                deform[3 * row_axis] * stress[pairing[0][col_axis]]
                + deform[3 * row_axis + 1] * stress[pairing[1][col_axis]]
                + deform[3 * row_axis + 2] * stress[pairing[2][col_axis]]
            )
    return jnp.stack(components)


def element_deform(extended):
    plane_low = extended[:, :-1]
    plane_high = extended[:, 1:]

    def roll_second(values):
        return jnp.roll(values, -1, axis=2)

    def roll_third(values):
        return jnp.roll(values, -1, axis=3)

    diff_first = plane_high - plane_low
    slope_first = 0.25 * (
        diff_first
        + roll_second(diff_first)
        + roll_third(diff_first)
        + roll_second(roll_third(diff_first))
    )
    plane_mid = 0.5 * (plane_low + plane_high)
    diff_second = roll_second(plane_mid) - plane_mid
    slope_second = 0.5 * (diff_second + roll_third(diff_second))
    diff_third = roll_third(plane_mid) - plane_mid
    slope_third = 0.5 * (diff_third + roll_second(diff_third))
    slopes = jnp.stack([slope_first, slope_second, slope_third], axis=1)
    identity = jnp.eye(3, dtype=extended.dtype)
    slopes = slopes + identity[:, :, None, None, None]
    return slopes.reshape(9, -1)


def nodal_force(piola, layout):
    tensor = piola.reshape((3, 3) + layout)
    planes = layout[0]
    nodal = jnp.zeros((3, planes + 1, layout[1], layout[2]), piola.dtype)
    for offset_plane in (0, 1):
        for offset_row in (0, 1):
            for offset_col in (0, 1):
                corner_term = 0.25 * (
                    (2 * offset_plane - 1) * tensor[:, 0]
                    + (2 * offset_row - 1) * tensor[:, 1]
                    + (2 * offset_col - 1) * tensor[:, 2]
                )
                corner_term = jnp.roll(
                    jnp.roll(corner_term, offset_row, axis=2), offset_col, axis=3
                )
                nodal = nodal.at[:, offset_plane : offset_plane + planes].add(corner_term)
    return nodal


def plan_kernel(old_ref, new_ref, steps_ref, source_ref, target_ref, order_ref, fill_ref, seen_ref):
    def clear(index, carry):
        seen_ref[index] = 0
        seen_ref[32 + index] = 0
        return carry

    lax.fori_loop(0, 32, clear, 0)

    def empty(index, carry):
        fill_ref[index] = 0
        return carry

    lax.fori_loop(0, NSUB, empty, 0)

    def place(element, carry):
        old = old_ref[element]
        rank = seen_ref[old]
        seen_ref[old] = rank + 1
        source_ref[element] = old * (8 * TILES) + rank
        new = new_ref[element]
        rank = seen_ref[32 + new]
        seen_ref[32 + new] = rank + 1
        target_ref[element] = new * (8 * TILES) + rank
        level = steps_ref[element] - 1
        position = fill_ref[level]
        fill_ref[level] = position + 1
        order_ref[level * POINTS + position] = element
        return carry

    lax.fori_loop(0, POINTS, place, 0)


def plan(old_owner, new_owner, substeps):
    smem = pl.BlockSpec(memory_space=pltpu.SMEM)
    return pl.pallas_call(
        plan_kernel,
        out_shape=(
            jax.ShapeDtypeStruct((POINTS,), jnp.int32),
            jax.ShapeDtypeStruct((POINTS,), jnp.int32),
            jax.ShapeDtypeStruct((NSUB * POINTS,), jnp.int32),
            jax.ShapeDtypeStruct((NSUB,), jnp.int32),
        ),
        in_specs=[smem] * 3,
        out_specs=(smem,) * 4,
        scratch_shapes=[pltpu.SMEM((64,), jnp.int32)],
        name="plan",
    )(old_owner, new_owner, substeps)


def row_part(start, quad):
    return pl.ds(start + 64 * quad, 8, stride=8)


def relax_kernel(
    source_ref,
    target_ref,
    order_ref,
    fill_ref,
    codes_ref,
    flow_ref,
    rate_ref,
    levels_ref,
    held_ref,
    sent_ref,
):
    sent_ref[...] = jnp.zeros_like(sent_ref)
    for steps in range(1, NSUB + 1):
        count = fill_ref[steps - 1]
        gains = []
        for quad in range(QUADS):
            rate = rate_ref[pl.ds(8 * quad, 8), :] * ((young + harden) / steps)
            gains.append(rate / (1.0 + rate))

        def pair(turn, carry, steps=steps, count=count, gains=gains):
            for member in range(2):
                position = jnp.minimum(2 * turn + member, count - 1)
                element = order_ref[(steps - 1) * POINTS + position]
                source = source_ref[element]
                target = target_ref[element]
                parts = [
                    held_ref[row_part(source, quad), :] * (young + harden)
                    for quad in range(QUADS)
                ]
                for step in range(steps):
                    level = jnp.broadcast_to(
                        levels_ref[pl.ds(step * POINTS + element, 1), :], (8, LANES)
                    )
                    for quad in range(QUADS):
                        stress = jnp.take_along_axis(
                            level, codes_ref[pl.ds(8 * quad, 8), :], axis=1
                        )
                        flow = flow_ref[pl.ds(8 * quad, 8), :]
                        trial = stress - parts[quad]
                        held = jnp.minimum(jnp.maximum(trial, -flow), flow)
                        parts[quad] = parts[quad] + (trial - held) * gains[quad]
                for quad in range(QUADS):
                    sent_ref[row_part(target, quad), :] = parts[quad] * (1.0 / (young + harden))
            return carry

        lax.fori_loop(0, (count + 1) // 2, pair, 0)


def relax(source, target, order, fill, codes, flow, rate, levels, held):
    smem = pl.BlockSpec(memory_space=pltpu.SMEM)
    vmem = pl.BlockSpec(memory_space=pltpu.VMEM)
    return pl.pallas_call(
        relax_kernel,
        out_shape=jax.ShapeDtypeStruct(held.shape, jnp.float32),
        in_specs=[smem] * 4 + [vmem] * 5,
        out_specs=vmem,
        compiler_params=pltpu.CompilerParams(vmem_limit_bytes=32 * 2**20),
        name="relax",
    )(source, target, order, fill, codes, flow, rate, levels, held)


def stress_kernel(target_ref, codes_ref, last_ref, basis_ref, sent_ref, sums_ref):
    def one(element, carry):
        target = target_ref[element]
        level = jnp.broadcast_to(last_ref[pl.ds(element, 1), :], (8, LANES))
        totals = [None] * 6
        for quad in range(QUADS):
            stress = jnp.take_along_axis(level, codes_ref[pl.ds(8 * quad, 8), :], axis=1)
            stress = stress - young * sent_ref[row_part(target, quad), :]
            for part in range(6):
                term = stress * basis_ref[pl.ds(part * TILES + 8 * quad, 8), :]
                totals[part] = term if quad == 0 else totals[part] + term
        for part in range(6):
            sums_ref[pl.ds(part * POINTS + element, 1), :] = jnp.sum(
                totals[part], axis=0, keepdims=True
            )
        return carry

    lax.fori_loop(0, POINTS, one, 0)


def cell_stress(target, codes, last, basis, sent):
    smem = pl.BlockSpec(memory_space=pltpu.SMEM)
    vmem = pl.BlockSpec(memory_space=pltpu.VMEM)
    sums = pl.pallas_call(
        stress_kernel,
        out_shape=jax.ShapeDtypeStruct((6 * POINTS, LANES), jnp.float32),
        in_specs=[smem] + [vmem] * 4,
        out_specs=vmem,
        compiler_params=pltpu.CompilerParams(vmem_limit_bytes=32 * 2**20),
        name="cell_stress",
    )(target, codes, last, basis, sent)
    return jnp.sum(sums, axis=1).reshape(6, POINTS) / STRUTS


def to_tiles(slots, owners):
    split = slots.reshape(owners, 8, TILES, LANES)
    return split.transpose(0, 2, 1, 3).reshape(owners, 8 * TILES, LANES)


def from_tiles(tiles, owners):
    split = tiles.reshape(owners, TILES, 8, LANES)
    return split.transpose(0, 2, 1, 3).reshape(owners * 8, STRUTS)


def shards(
    displacement,
    velocity,
    old_owner,
    new_owner,
    substeps,
    strut_ends,
    flow_stress,
    relax_rate,
    plastic_old,
):
    owners = lax.axis_size("rve")
    planes = displacement.shape[1]
    displacement_next = displacement + time_step * velocity
    both = jnp.concatenate([displacement, displacement_next], axis=0)
    rim = from_behind(both, ("macro", "rve"), -1)
    held = lax.all_to_all(to_tiles(plastic_old, owners), "rve", split_axis=0, concat_axis=0, tiled=True)
    held = held.reshape(owners * 8 * TILES, LANES)

    source, target, order, fill = plan(old_owner.reshape(-1), new_owner.reshape(-1), substeps)
    codes = direction_codes(strut_ends)
    products = jnp.asarray(direction_products())
    extended = jnp.concatenate([both, rim], axis=1)
    deform_old = element_deform(extended[:3])
    deform_new = element_deform(extended[3:])
    counts = substeps.astype(jnp.float32)
    change = deform_new - deform_old
    doubled = jnp.asarray(np.array([1, 1, 1, 2, 2, 2], np.float32))[:, None] * products
    turns = jnp.arange(1, NSUB + 1, dtype=jnp.float32)[:, None]
    fraction = jnp.minimum(turns, counts[None, :]) / counts[None, :]
    path = deform_old[:, None, :] + fraction[None] * change[:, None, :]
    levels = young * jnp.einsum("cje,cd->jed", green(path), doubled, precision=highest)
    last = levels[NSUB - 1]
    levels = levels.reshape(NSUB * POINTS, LANES)
    flow = flow_stress.reshape(TILES, LANES)
    rate = relax_rate.reshape(TILES, LANES)
    sent = relax(source, target, order, fill, codes, flow, rate, levels, held)

    moved = lax.all_to_all(
        sent.reshape(owners, 8 * TILES, LANES), "rve", split_axis=0, concat_axis=0, tiled=True
    )
    plastic_new = from_tiles(moved, owners)

    basis = jnp.take(products, codes.reshape(-1), axis=1).reshape(6 * TILES, LANES)
    stress = cell_stress(target, codes, last, basis, sent)
    piola = first_stress(deform_new, stress)
    nodal = nodal_force(piola, (planes, displacement.shape[2], displacement.shape[3]))
    carried = from_behind(nodal[:, planes:], ("macro", "rve"), 1)
    interior = nodal[:, :planes].at[:, :1].add(carried)
    velocity_next = velocity - time_step * interior
    return (displacement_next, velocity_next, plastic_new)


def solution(mesh):
    in_specs = (
        P(None, ("macro", "rve"), None, None),
        P(None, ("macro", "rve"), None, None),
        P(("macro", "rve"), None),
        P(("macro", "rve"), None),
        P(("macro", "rve")),
        P(),
        P(),
        P(),
        P(("macro", "rve"), None),
    )
    out_specs = (
        P(None, ("macro", "rve"), None, None),
        P(None, ("macro", "rve"), None, None),
        P(("macro", "rve"), None),
    )
    return jax.shard_map(shards, mesh=mesh, in_specs=in_specs, out_specs=out_specs, check_vma=False)
```

time: 245 us -> 151 us (0.62)
  matrix products: 80.8 us -> 1 us
  waiting for transfers between devices: 106 us -> 70.5 us
  Pallas kernels: 0 us -> 29.3 us
  starting transfers between devices: 27.2 us -> 19.7 us
    dot_general x10 -> x1, matrix products: 80.8 us -> 1 us  [shards(): jnp.einsum('cje,cd->jed', green(path), doubled, precision=highest)]
    pallas_call x0 -> x3, Pallas kernels: none -> 29.3 us  [the longest x1 13.9 us: relax(): pl.pallas_call(relax_kernel, out_shape=jax.ShapeDtypeStruct(held.shape, j...]
    ppermute x3 -> x2, waiting for transfers between devices: 44.2 us -> 19.1 us  [from_behind(): lax.ppermute(value, axis, [(source, source + steps) for source in range(i...]
    all_to_all x3 -> x2, waiting for transfers between devices: 62.2 us -> 51.4 us  [the longest x1 46.9 us: shards(): lax.all_to_all(to_tiles(plastic_old, owners), 'rve', split_axis=0, concat...]
    gather x1 -> x3, local copies, waits for them, and re-layouts: 4.42 us -> 11.5 us  [shards(): jnp.take(products, codes.reshape(-1), axis=1).reshape(6 * TILES, LANES)]
    scatter x2 -> x0, local copies, waits for them, and re-layouts: 4.89 us -> none  [the longest x1 3.98 us: shards(): moving = jnp.zeros_like(plastic_old).at[new_slots].set(plastic)]
    all_to_all x3 -> x2, starting transfers between devices: 14.8 us -> 10 us  [the longest x1 5.01 us: shards(): lax.all_to_all(to_tiles(plastic_old, owners), 'rve', split_axis=0, concat...]
    ppermute x3 -> x2, starting transfers between devices: 12.4 us -> 9.74 us  [from_behind(): lax.ppermute(value, axis, [(source, source + steps) for source in range(i...]
  transfers between devices with their start and end apart: 6 -> 4, of which waited for: 4 -> 3; matrix products, arithmetic and copies ran while one was open for 3% -> 11% of each run, Pallas kernels for 0% -> 10%
where the time goes in v1:
time: 151 us; the launch traced here: 150 us
  waiting for transfers between devices  70.5 us (47%)
  Pallas kernels  29.3 us (19%)
  local copies, waits for them, and re-layouts  24 us (16%)
  starting transfers between devices  19.7 us (13%)
  other arithmetic  4.42 us (3%)
    all_to_all x1, waiting for transfers between devices, shards(): lax.all_to_all(to_tiles(plastic_old, owners), 'rve', split_axis=0, concat...  46.9 us
    ppermute x2, waiting for transfers between devices, from_behind(): lax.ppermute(value, axis, [(source, source + steps) for source in range(i...  19.1 us
    pallas_call x1, Pallas kernels, relax(): pl.pallas_call(relax_kernel, out_shape=jax.ShapeDtypeStruct(held.shape, j...  13.9 us
    pallas_call x1, Pallas kernels, cell_stress(): pl.pallas_call(stress_kernel, out_shape=jax.ShapeDtypeStruct((6 * POINTS,...  11.9 us
    unnamed x33, local copies, waits for them, and re-layouts  11.5 us
    gather x3, local copies, waits for them, and re-layouts, shards(): jnp.take(products, codes.reshape(-1), axis=1).reshape(6 * TILES, LANES)  11.5 us
    ppermute x2, starting transfers between devices, from_behind(): lax.ppermute(value, axis, [(source, source + steps) for source in range(i...  9.74 us
    all_to_all x1, starting transfers between devices, shards(): lax.all_to_all(to_tiles(plastic_old, owners), 'rve', split_axis=0, concat...  5.01 us
  transfers between devices with their start and end apart: 4, of which 3 were waited for; matrix products, arithmetic and copies ran while one was open for 11% of the time, Pallas kernels for 10%

profile of v1, /device:TPU:24, one launch (start us, length us, event | category | flops | bytes accessed | tf_op | source)
XLA Modules:
  0.0 150.1 jit_solution(475429427382218469)
XLA Ops:
  0.6 0.7 multiply_add_fusion.1
  1.4 0.7 pad_maximum_fusion.2
  2.1 7.7 %collective-permute-start = (f32[6,1,8,16]{3,2,0,1:T(8,128)S(1)}, f32[6,1,8,16]{3,2,0,1:T(8,128)S(1)}, u32[]{:S(2)}, u32[]{:S(2)}) collective-permute-start(f32[6,1,8,16]{3,2,0,1:T(8,128)S(1)} %pad_maximum_fusion.2), channel_id=1, source_target_pairs={{1,0},{2,1},{3,2},{4,3},{5,4},{6,5},{7,6},{8,7},{9,8},{10,9},{11,1... | collective-permute-start | bytes 9224 | tf_op jit(solution)/shard_map/ppermute | solution.py:28
  9.9 5.0 %all-to-all-start = ((f32[32,256,128]{2,1,0:T(8,128)}), f32[32,256,128]{2,1,0:T(8,128)}, u32[]{:S(2)}, u32[]{:S(2)}) async-start(f32[32,256,128]{2,1,0:T(8,128)} %bitcast.308), calls=%async_computation | async-start | bytes 8388608 | tf_op jit(solution)/shard_map/all_to_all | solution.py:310
  15.0 0.1 compare_and_fusion
  15.2 0.1 reshape.1371
  15.3 3.5 %plan.1 = (s32[128]{0:T(128)}, s32[128]{0:T(128)}, s32[1024]{0:T(1024)}, s32[8]{0:T(128)}) custom-call(s32[128]{0:T(128)} %bitcast.335, s32[128]{0:T(128)} %bitcast.336, s32[128]{0:T(128)} %steps_ref.1), custom_call_target="tpu_custom_call" | custom-call | tf_op jit(solution)/shard_map/plan/pallas_call | solution.py:169
  18.8 0.1 slice.713
  18.9 0.1 slice.695
  19.0 0.1 maximum_subtract_fusion.2
  19.0 0.1 maximum_subtract_fusion.1
  19.1 0.1 slice.685
  19.3 0.1 slice.711
  19.4 0.1 fusion.70
  19.5 0.1 fusion.69
  19.6 0.1 slice_maximum_fusion.3
  19.6 0.1 slice_maximum_fusion.2
  19.7 0.1 fusion.62
  19.8 0.1 fusion.54
  19.9 0.1 stack.58
  20.0 0.1 slice.693
  20.1 0.1 fusion.56
  20.2 0.1 stack.53
  20.3 0.1 fusion.90
  20.5 1.0 convolution_multiply_fusion
  21.5 46.9 %all-to-all-done = f32[32,256,128]{2,1,0:T(8,128)} async-done(((f32[32,256,128]{2,1,0:T(8,128)}), f32[32,256,128]{2,1,0:T(8,128)}, u32[]{:S(2)}, u32[]{:S(2)}) %all-to-all-start) | async-done | bytes 4194336 | tf_op jit(solution)/shard_map/all_to_all | solution.py:310
  68.4 0.7 copy-done.4
  69.1 0.6 copy-done.5
  69.7 0.7 copy-done.7
  70.3 0.7 copy-done.8
  71.0 13.9 %relax.1.sent_ref = f32[8192,128]{1,0:T(8,128)S(1)} custom-call(s32[128]{0:T(128)S(1)} %copy-done.7, s32[128]{0:T(128)S(1)} %copy-done.5, s32[1024]{0:T(1024)S(1)} %copy-done.4, s32[8]{0:T(128)S(1)} %copy-done.8, s32[32,128]{1,0:T(8,128)S(1)} %get-tuple-element.128.codes_ref, f32[32,128]{1,0:T(8,128)S(1)} %bitcast.306, f32[32,128]{1,0:T(8,128)S(1)} %bitcast.307, ...), custom_call_target="tpu_custom_call" | custom-call | tf_op jit(solution)/shard_map/relax/pallas_call | solution.py:240
  84.9 2.0 %copy-done = f32[8192,128]{1,0:T(8,128)} copy-done((f32[8192,128]{1,0:T(8,128)}, f32[8192,128]{1,0:T(8,128)S(1)}, u32[]{:S(2)}) %copy-start) | copy-done | bytes 4194328
  87.0 5.0 %all-to-all-start.1 = ((f32[32,256,128]{2,1,0:T(8,128)}), f32[32,256,128]{2,1,0:T(8,128)}, u32[]{:S(2)}, u32[]{:S(2)}) async-start(f32[32,256,128]{2,1,0:T(8,128)} %bitcast.304), calls=%async_computation.1 | async-start | bytes 8388608 | tf_op jit(solution)/shard_map/all_to_all | solution.py:332
  92.0 0.7 compare_select_fusion
  92.7 10.8 %gather_fusion = f32[4096,6]{1,0:T(8,128)S(1)} fusion(f32[6,128]{0,1:T(8,128)S(1)} %copy-done.9, s32[4096]{0:T(1024)S(1)} %broadcast_clamp_fusion), kind=kCustom, calls=%fused_computation | custom fusion | bytes 212992 | tf_op jit(solution)/shard_map/jit(_take)/gather | solution.py:337
  103.5 0.6 copy.64
  104.3 2.2 %copy-done.1 = f32[8192,128]{1,0:T(8,128)S(1)} copy-done((f32[8192,128]{1,0:T(8,128)S(1)}, f32[8192,128]{1,0:T(8,128)}, u32[]{:S(2)}) %copy-start.1) | copy-done | bytes 4194328
  106.4 11.9 %cell_stress.1 = f32[768,128]{1,0:T(8,128)S(1)} custom-call(s32[128]{0:T(128)S(1)} %copy-done.6, s32[32,128]{1,0:T(8,128)S(1)} %get-tuple-element.128.codes_ref, f32[128,128]{1,0:T(8,128)S(1)} %slice_bitcast_fusion.last_ref, f32[192,128]{1,0:T(8,128)S(1)} %bitcast_select_fusion.basis_ref, f32[8192,128]{1,0:T(8,128)S(1)} %copy-done.1), custom_call_target="tpu_custom_call" | custom-call | tf_op jit(solution)/shard_map/cell_stress/pallas_call | solution.py:273
  118.4 0.2 reduce_sum.9
  118.7 0.1 reshape.1367
  118.9 0.1 slice_maximum_fusion
  118.9 0.1 fusion.44
  119.0 2.0 %collective-permute-start.1 = (f32[3,1,8,16]{3,2,0,1:T(8,128)S(1)}, f32[3,1,8,16]{3,2,0,1:T(8,128)S(1)}, u32[]{:S(2)}, u32[]{:S(2)}) collective-permute-start(f32[3,1,8,16]{3,2,0,1:T(8,128)S(1)} %fusion.44), channel_id=1, source_target_pairs={{0,1},{1,2},{2,3},{3,4},{4,5},{5,6},{6,7},{7,8},{8,9},{9,10},{10,1... | collective-permute-start | bytes 4616 | tf_op jit(solution)/shard_map/ppermute | solution.py:28
  121.0 0.1 slice_maximum_fusion.1
  121.2 19.1 %collective-permute-done.1 = f32[3,1,8,16]{3,2,0,1:T(8,128)S(1)} collective-permute-done((f32[3,1,8,16]{3,2,0,1:T(8,128)S(1)}, f32[3,1,8,16]{3,2,0,1:T(8,128)S(1)}, u32[]{:S(2)}, u32[]{:S(2)}) %collective-permute-start.1) | collective-permute-done | bytes 1568 | tf_op jit(solution)/shard_map/ppermute | solution.py:28
  140.2 0.7 fusion.50
  140.9 4.5 %all-to-all-done.1 = f32[32,256,128]{2,1,0:T(8,128)} async-done(((f32[32,256,128]{2,1,0:T(8,128)}), f32[32,256,128]{2,1,0:T(8,128)}, u32[]{:S(2)}, u32[]{:S(2)}) %all-to-all-start.1) | async-done | bytes 4194336 | tf_op jit(solution)/shard_map/all_to_all | solution.py:332
  145.4 4.7 %copy.80 = f32[256,4096]{1,0:T(8,128)} copy(f32[256,4096]{1,0:T(8,128)} %bitcast.48) | data formatting | bytes 8388608
  (77 shorter events, 0.8 us)
Async XLA Ops:
  1.4 17.5 %copy-start.10 = (f32[3,1,8,16]{3,2,1,0:T(8,128)}, f32[3,1,8,16]{3,2,1,0:T(8,128)S(1)}, u32[]{:S(2)}) copy-start(f32[3,1,8,16]{3,2,1,0:T(8,128)S(1)} %multiply_add_fusion.1) | copy-start | bytes 4612
  2.1 16.7 %collective-permute-start = (f32[6,1,8,16]{3,2,0,1:T(8,128)S(1)}, f32[6,1,8,16]{3,2,0,1:T(8,128)S(1)}, u32[]{:S(2)}, u32[]{:S(2)}) collective-permute-start(f32[6,1,8,16]{3,2,0,1:T(8,128)S(1)} %pad_maximum_fusion.2), channel_id=1, source_target_pairs={{1,0},{2,1},{3,2},{4,3},{5,4},{6,5},{7,6},{8,7},{9,8},{10,9},{11,1... | collective-permute-start | bytes 9224 | tf_op jit(solution)/shard_map/ppermute | solution.py:28
  9.8 5.1 %copy-start.11 = (s32[2,4096]{1,0:T(2,128)S(1)}, s32[2,4096]{1,0:T(2,128)}, u32[]{:S(2)}) copy-start(s32[2,4096]{1,0:T(2,128)} %param.36) | copy-start | bytes 98308
  9.8 5.1 %copy-start.15 = (s32[128]{0:T(128)S(1)}, s32[128]{0:T(128)}, u32[]{:S(2)}) copy-start(s32[128]{0:T(128)} %steps_ref.1) | copy-start | bytes 1540
  9.9 8.9 %copy-start.12 = (f32[3,1,8,16]{3,2,1,0:T(8,128)S(1)}, f32[3,1,8,16]{3,2,1,0:T(8,128)}, u32[]{:S(2)}) copy-start(f32[3,1,8,16]{3,2,1,0:T(8,128)} %param.31) | copy-start | bytes 4612
  9.9 10.6 %copy-start.14 = (f32[6,128,1]{1,0,2:T(8,128)S(1)}, f32[6,128,1]{1,0,2:T(8,128)}, u32[]{:S(2)}) copy-start(f32[6,128,1]{1,0,2:T(8,128)} %constant.426) | copy-start | bytes 9220
  9.9 58.5 %copy-start.2 = (f32[4096]{0:T(1024)S(1)}, f32[4096]{0:T(1024)}, u32[]{:S(2)}) copy-start(f32[4096]{0:T(1024)} %param.37) | copy-start | bytes 49156
  9.9 58.5 %copy-start.3 = (f32[4096]{0:T(1024)S(1)}, f32[4096]{0:T(1024)}, u32[]{:S(2)}) copy-start(f32[4096]{0:T(1024)} %param.38) | copy-start | bytes 49156
  9.9 58.5 %all-to-all-start = ((f32[32,256,128]{2,1,0:T(8,128)}), f32[32,256,128]{2,1,0:T(8,128)}, u32[]{:S(2)}, u32[]{:S(2)}) async-start(f32[32,256,128]{2,1,0:T(8,128)} %bitcast.308), calls=%async_computation | async-start | bytes 8388608 | tf_op jit(solution)/shard_map/all_to_all | solution.py:310
  68.4 0.7 copy-start.4
  69.1 0.6 copy-start.5
  69.7 0.7 copy-start.7
  70.3 0.7 copy-start.8
  84.9 2.0 %copy-start = (f32[8192,128]{1,0:T(8,128)}, f32[8192,128]{1,0:T(8,128)S(1)}, u32[]{:S(2)}) copy-start(f32[8192,128]{1,0:T(8,128)S(1)} %relax.1.sent_ref) | copy-start | bytes 12582916
  87.0 5.8 %copy-start.9 = (f32[6,128]{0,1:T(8,128)S(1)}, f32[6,128]{0,1:T(8,128)}, u32[]{:S(2)}) copy-start(f32[6,128]{0,1:T(8,128)} %constant.421.clone) | copy-start | bytes 9220
  87.0 17.3 %copy-start.6 = (s32[128]{0:T(128)S(1)}, s32[128]{0:T(128)}, u32[]{:S(2)}) copy-start(s32[128]{0:T(128)} %get-tuple-element.123.target_ref) | copy-start | bytes 1540
  87.0 58.5 %all-to-all-start.1 = ((f32[32,256,128]{2,1,0:T(8,128)}), f32[32,256,128]{2,1,0:T(8,128)}, u32[]{:S(2)}, u32[]{:S(2)}) async-start(f32[32,256,128]{2,1,0:T(8,128)} %bitcast.304), calls=%async_computation.1 | async-start | bytes 8388608 | tf_op jit(solution)/shard_map/all_to_all | solution.py:332
  103.5 36.7 %copy-start.13 = (f32[3,1,8,16]{3,2,1,0:T(8,128)S(1)}, f32[3,1,8,16]{3,2,1,0:T(8,128)}, u32[]{:S(2)}) copy-start(f32[3,1,8,16]{3,2,1,0:T(8,128)} %param.32) | copy-start | bytes 4612
  104.2 2.2 %copy-start.1 = (f32[8192,128]{1,0:T(8,128)S(1)}, f32[8192,128]{1,0:T(8,128)}, u32[]{:S(2)}) copy-start(f32[8192,128]{1,0:T(8,128)} %copy-done) | copy-start | bytes 12582916
  119.0 21.2 %collective-permute-start.1 = (f32[3,1,8,16]{3,2,0,1:T(8,128)S(1)}, f32[3,1,8,16]{3,2,0,1:T(8,128)S(1)}, u32[]{:S(2)}, u32[]{:S(2)}) collective-permute-start(f32[3,1,8,16]{3,2,0,1:T(8,128)S(1)} %fusion.44), channel_id=1, source_target_pairs={{0,1},{1,2},{2,3},{3,4},{4,5},{5,6},{6,7},{7,8},{8,9},{9,10},{10,1... | collective-permute-start | bytes 4616 | tf_op jit(solution)/shard_map/ppermute | solution.py:28

commit v2 on v1

--- a/solution.py
+++ b/solution.py
@@ -14,7 +14,10 @@
 LANES = 128
 POINTS = 128
 TILES = STRUTS // LANES
-QUADS = TILES // 8
+OWNERS = 32
+CAP = 8
+GROUP = 8
+SPAN = 2
 
 young = 10.0
 harden = 1.0
@@ -132,33 +135,39 @@
     return nodal
 
 
-def plan_kernel(old_ref, new_ref, steps_ref, source_ref, target_ref, order_ref, fill_ref, seen_ref):
+def plan_kernel(old_ref, new_ref, steps_ref, plan_ref, seen_ref):
     def clear(index, carry):
         seen_ref[index] = 0
-        seen_ref[32 + index] = 0
         return carry
 
-    lax.fori_loop(0, 32, clear, 0)
-
-    def empty(index, carry):
-        fill_ref[index] = 0
+    lax.fori_loop(0, 2 * OWNERS + NSUB + 1, clear, 0)
+
+    def count(element, carry):
+        level = 2 * OWNERS + steps_ref[element]
+        seen_ref[level] = seen_ref[level] + 1
         return carry
 
-    lax.fori_loop(0, NSUB, empty, 0)
+    lax.fori_loop(0, POINTS, count, 0)
+    start = 0
+    for steps in range(NSUB + 1):
+        held = seen_ref[2 * OWNERS + steps]
+        seen_ref[2 * OWNERS + steps] = start
+        plan_ref[3 * POINTS + steps] = start + held
+        start = start + held
 
     def place(element, carry):
         old = old_ref[element]
-        rank = seen_ref[old]
-        seen_ref[old] = rank + 1
-        source_ref[element] = old * (8 * TILES) + rank
-        new = new_ref[element]
-        rank = seen_ref[32 + new]
-        seen_ref[32 + new] = rank + 1
-        target_ref[element] = new * (8 * TILES) + rank
-        level = steps_ref[element] - 1
-        position = fill_ref[level]
-        fill_ref[level] = position + 1
-        order_ref[level * POINTS + position] = element
+        old_rank = seen_ref[old]
+        seen_ref[old] = old_rank + 1
+        new = OWNERS + new_ref[element]
+        new_rank = seen_ref[new]
+        seen_ref[new] = new_rank + 1
+        level = 2 * OWNERS + steps_ref[element]
+        position = seen_ref[level]
+        seen_ref[level] = position + 1
+        plan_ref[position] = element
+        plan_ref[POINTS + position] = old * CAP + old_rank
+        plan_ref[2 * POINTS + position] = (new - OWNERS) * CAP + new_rank
         return carry
 
     lax.fori_loop(0, POINTS, place, 0)
@@ -168,93 +177,89 @@
     smem = pl.BlockSpec(memory_space=pltpu.SMEM)
     return pl.pallas_call(
         plan_kernel,
-        out_shape=(
-            jax.ShapeDtypeStruct((POINTS,), jnp.int32),
-            jax.ShapeDtypeStruct((POINTS,), jnp.int32),
-            jax.ShapeDtypeStruct((NSUB * POINTS,), jnp.int32),
-            jax.ShapeDtypeStruct((NSUB,), jnp.int32),
-        ),
+        out_shape=jax.ShapeDtypeStruct((4 * POINTS,), jnp.int32),
         in_specs=[smem] * 3,
-        out_specs=(smem,) * 4,
-        scratch_shapes=[pltpu.SMEM((64,), jnp.int32)],
+        out_specs=smem,
+        scratch_shapes=[pltpu.SMEM((2 * OWNERS + NSUB + 1,), jnp.int32)],
         name="plan",
     )(old_owner, new_owner, substeps)
 
 
-def row_part(start, quad):
-    return pl.ds(start + 64 * quad, 8, stride=8)
-
-
-def relax_kernel(
-    source_ref,
-    target_ref,
-    order_ref,
-    fill_ref,
-    codes_ref,
-    flow_ref,
-    rate_ref,
-    levels_ref,
-    held_ref,
-    sent_ref,
-):
+def row_part(row, part):
+    return row >> 3, pl.ds(8 * CAP * part + (row & 7), 8, stride=CAP), slice(None)
+
+
+def relax_kernel(plan_ref, codes_ref, flow_ref, rate_ref, levels_ref, held_ref, sent_ref):
     sent_ref[...] = jnp.zeros_like(sent_ref)
+    parts = [pl.ds(8 * part, 8) for part in range(SPAN)]
     for steps in range(1, NSUB + 1):
-        count = fill_ref[steps - 1]
+        first = plan_ref[3 * POINTS + steps - 1]
+        end = plan_ref[3 * POINTS + steps]
         gains = []
-        for quad in range(QUADS):
-            rate = rate_ref[pl.ds(8 * quad, 8), :] * ((young + harden) / steps)
+        for part in parts:
+            rate = rate_ref[part, :] * ((young + harden) / steps)
             gains.append(rate / (1.0 + rate))
 
-        def pair(turn, carry, steps=steps, count=count, gains=gains):
-            for member in range(2):
-                position = jnp.minimum(2 * turn + member, count - 1)
-                element = order_ref[(steps - 1) * POINTS + position]
-                source = source_ref[element]
-                target = target_ref[element]
-                parts = [
-                    held_ref[row_part(source, quad), :] * (young + harden)
-                    for quad in range(QUADS)
-                ]
-                for step in range(steps):
+        def group(turn, carry, steps=steps, first=first, end=end, gains=gains):
+            places = [jnp.minimum(first + GROUP * turn + i, end - 1) for i in range(GROUP)]
+            elements = [plan_ref[place] for place in places]
+            sources = [plan_ref[POINTS + place] for place in places]
+            targets = [plan_ref[2 * POINTS + place] for place in places]
+            state = [
+                [held_ref[row_part(source, part)] * (young + harden) for part in range(SPAN)]
+                for source in sources
+            ]
+            for step in range(steps):
+                for i in range(GROUP):
                     level = jnp.broadcast_to(
-                        levels_ref[pl.ds(step * POINTS + element, 1), :], (8, LANES)
+                        levels_ref[pl.ds(step * POINTS + elements[i], 1), :], (8, LANES)
                     )
-                    for quad in range(QUADS):
-                        stress = jnp.take_along_axis(
-                            level, codes_ref[pl.ds(8 * quad, 8), :], axis=1
-                        )
-                        flow = flow_ref[pl.ds(8 * quad, 8), :]
-                        trial = stress - parts[quad]
+                    for part in range(SPAN):
+                        stress = jnp.take_along_axis(level, codes_ref[parts[part], :], axis=1)
+                        flow = flow_ref[parts[part], :]
+                        trial = stress - state[i][part]
                         held = jnp.minimum(jnp.maximum(trial, -flow), flow)
-                        parts[quad] = parts[quad] + (trial - held) * gains[quad]
-                for quad in range(QUADS):
-                    sent_ref[row_part(target, quad), :] = parts[quad] * (1.0 / (young + harden))
+                        state[i][part] = state[i][part] + (trial - held) * gains[part]
+            for i in range(GROUP):
+                for part in range(SPAN):
+                    sent_ref[row_part(targets[i], part)] = state[i][part] * (
+                        1.0 / (young + harden)
+                    )
             return carry
 
-        lax.fori_loop(0, (count + 1) // 2, pair, 0)
-
-
-def relax(source, target, order, fill, codes, flow, rate, levels, held):
-    smem = pl.BlockSpec(memory_space=pltpu.SMEM)
-    vmem = pl.BlockSpec(memory_space=pltpu.VMEM)
+        lax.fori_loop(0, (end - first + GROUP - 1) // GROUP, group, 0)
+
+
+def relax(order, codes, flow, rate, levels, held):
+    strip = pl.BlockSpec((8 * SPAN, LANES), lambda turn: (turn, 0))
+    rows = pl.BlockSpec((OWNERS, 8 * SPAN * CAP, LANES), lambda turn: (0, turn, 0))
     return pl.pallas_call(
         relax_kernel,
         out_shape=jax.ShapeDtypeStruct(held.shape, jnp.float32),
-        in_specs=[smem] * 4 + [vmem] * 5,
-        out_specs=vmem,
+        grid=(TILES // (8 * SPAN),),
+        in_specs=[
+            pl.BlockSpec(memory_space=pltpu.SMEM),
+            strip,
+            strip,
+            strip,
+            pl.BlockSpec(memory_space=pltpu.VMEM),
+            rows,
+        ],
+        out_specs=rows,
         compiler_params=pltpu.CompilerParams(vmem_limit_bytes=32 * 2**20),
         name="relax",
-    )(source, target, order, fill, codes, flow, rate, levels, held)
-
-
-def stress_kernel(target_ref, codes_ref, last_ref, basis_ref, sent_ref, sums_ref):
-    def one(element, carry):
-        target = target_ref[element]
+    )(order, codes, flow, rate, levels, held)
+
+
+def stress_kernel(plan_ref, codes_ref, last_ref, basis_ref, sent_ref, sums_ref):
+    def one(place, carry):
+        element = plan_ref[place]
+        target = plan_ref[2 * POINTS + place]
         level = jnp.broadcast_to(last_ref[pl.ds(element, 1), :], (8, LANES))
         totals = [None] * 6
-        for quad in range(QUADS):
+        for quad in range(TILES // 8):
             stress = jnp.take_along_axis(level, codes_ref[pl.ds(8 * quad, 8), :], axis=1)
-            stress = stress - young * sent_ref[row_part(target, quad), :]
+            stress = stress - young * sent_ref[row_part(target, quad)]
             for part in range(6):
                 term = stress * basis_ref[pl.ds(part * TILES + 8 * quad, 8), :]
                 totals[part] = term if quad == 0 else totals[part] + term
@@ -267,7 +272,7 @@
     lax.fori_loop(0, POINTS, one, 0)
 
 
-def cell_stress(target, codes, last, basis, sent):
+def cell_stress(order, codes, last, basis, sent):
     smem = pl.BlockSpec(memory_space=pltpu.SMEM)
     vmem = pl.BlockSpec(memory_space=pltpu.VMEM)
     sums = pl.pallas_call(
@@ -277,18 +282,37 @@
         out_specs=vmem,
         compiler_params=pltpu.CompilerParams(vmem_limit_bytes=32 * 2**20),
         name="cell_stress",
-    )(target, codes, last, basis, sent)
+    )(order, codes, last, basis, sent)
     return jnp.sum(sums, axis=1).reshape(6, POINTS) / STRUTS
 
 
-def to_tiles(slots, owners):
-    split = slots.reshape(owners, 8, TILES, LANES)
-    return split.transpose(0, 2, 1, 3).reshape(owners, 8 * TILES, LANES)
-
-
-def from_tiles(tiles, owners):
-    split = tiles.reshape(owners, TILES, 8, LANES)
-    return split.transpose(0, 2, 1, 3).reshape(owners * 8, STRUTS)
+def hand_over(slots):
+    def kernel(received_ref, result_ref):
+        result_ref[...] = received_ref[...]
+
+    rows = pl.BlockSpec((slots.shape[0] // 8, slots.shape[1]), lambda turn: (turn, 0))
+    return pl.pallas_call(
+        kernel,
+        out_shape=jax.ShapeDtypeStruct(slots.shape, slots.dtype),
+        grid=(8,),
+        in_specs=[rows],
+        out_specs=rows,
+        name="hand_over",
+    )(slots)
+
+
+def to_tiles(slots):
+    split = slots.reshape(OWNERS, CAP, TILES, LANES)
+    return split.transpose(0, 2, 1, 3).reshape(OWNERS, TILES * CAP, LANES)
+
+
+def from_tiles(tiles):
+    split = tiles.reshape(OWNERS, TILES, CAP, LANES)
+    return split.transpose(0, 2, 1, 3).reshape(OWNERS * CAP, STRUTS)
+
+
+def exchange(blocks):
+    return lax.all_to_all(blocks, "rve", split_axis=0, concat_axis=0, tiled=True)
 
 
 def shards(
@@ -302,20 +326,18 @@
     relax_rate,
     plastic_old,
 ):
-    owners = lax.axis_size("rve")
     planes = displacement.shape[1]
+    both = jnp.concatenate([displacement, velocity], axis=0)
+    rim = from_behind(both, ("macro", "rve"), -1)
+    held = exchange(to_tiles(plastic_old))
+
     displacement_next = displacement + time_step * velocity
-    both = jnp.concatenate([displacement, displacement_next], axis=0)
-    rim = from_behind(both, ("macro", "rve"), -1)
-    held = lax.all_to_all(to_tiles(plastic_old, owners), "rve", split_axis=0, concat_axis=0, tiled=True)
-    held = held.reshape(owners * 8 * TILES, LANES)
-
-    source, target, order, fill = plan(old_owner.reshape(-1), new_owner.reshape(-1), substeps)
+    rim_next = rim[:3] + time_step * rim[3:]
+    order = plan(old_owner.reshape(-1), new_owner.reshape(-1), substeps)
     codes = direction_codes(strut_ends)
     products = jnp.asarray(direction_products())
-    extended = jnp.concatenate([both, rim], axis=1)
-    deform_old = element_deform(extended[:3])
-    deform_new = element_deform(extended[3:])
+    deform_old = element_deform(jnp.concatenate([displacement, rim[:3]], axis=1))
+    deform_new = element_deform(jnp.concatenate([displacement_next, rim_next], axis=1))
     counts = substeps.astype(jnp.float32)
     change = deform_new - deform_old
     doubled = jnp.asarray(np.array([1, 1, 1, 2, 2, 2], np.float32))[:, None] * products
@@ -327,15 +349,12 @@
     levels = levels.reshape(NSUB * POINTS, LANES)
     flow = flow_stress.reshape(TILES, LANES)
     rate = relax_rate.reshape(TILES, LANES)
-    sent = relax(source, target, order, fill, codes, flow, rate, levels, held)
-
-    moved = lax.all_to_all(
-        sent.reshape(owners, 8 * TILES, LANES), "rve", split_axis=0, concat_axis=0, tiled=True
-    )
-    plastic_new = from_tiles(moved, owners)
+    sent = relax(order, codes, flow, rate, levels, held)
+
+    plastic_new = hand_over(from_tiles(exchange(sent)))
 
     basis = jnp.take(products, codes.reshape(-1), axis=1).reshape(6 * TILES, LANES)
-    stress = cell_stress(target, codes, last, basis, sent)
+    stress = cell_stress(order, codes, last, basis, sent)
     piola = first_stress(deform_new, stress)
     nodal = nodal_force(piola, (planes, displacement.shape[2], displacement.shape[3]))
     carried = from_behind(nodal[:, planes:], ("macro", "rve"), 1)

time: 151 us -> 145 us (0.960)
  local copies, waits for them, and re-layouts: 24 us -> 17.4 us
  Pallas kernels: 29.3 us -> 32.5 us
  waiting for transfers between devices: 70.5 us -> 68.3 us
    pallas_call x1 -> x2, Pallas kernels: 3.45 us -> 12.2 us  [the longest x1 6.58 us: hand_over(): pl.pallas_call(kernel, out_shape=jax.ShapeDtypeStruct(slots.shape, slots....]
    unnamed x33 -> x26, local copies, waits for them, and re-layouts: 11.5 us -> 4.93 us
    pallas_call x1, Pallas kernels: 13.9 us -> 8.37 us  [relax(): pl.pallas_call(relax_kernel, out_shape=jax.ShapeDtypeStruct(held.shape, j...]
    all_to_all x2, waiting for transfers between devices: 51.4 us -> 49 us  [exchange(): lax.all_to_all(blocks, 'rve', split_axis=0, concat_axis=0, tiled=True)]
  transfers between devices with their start and end apart: 4 -> 4, of which waited for: 3 -> 3; matrix products, arithmetic and copies ran while one was open for 11% -> 11% of each run, Pallas kernels for 10% -> 12%
where the time goes in v2:
time: 145 us; the launch traced here: 144 us
  waiting for transfers between devices  68.3 us (47%)
  Pallas kernels  32.5 us (22%)
  starting transfers between devices  19.7 us (14%)
  local copies, waits for them, and re-layouts  17.4 us (12%)
  other arithmetic  3.71 us (3%)
    all_to_all x2, waiting for transfers between devices, exchange(): lax.all_to_all(blocks, 'rve', split_axis=0, concat_axis=0, tiled=True)  49 us
    ppermute x2, waiting for transfers between devices, from_behind(): lax.ppermute(value, axis, [(source, source + steps) for source in range(i...  19.3 us
    pallas_call x1, Pallas kernels, cell_stress(): pl.pallas_call(stress_kernel, out_shape=jax.ShapeDtypeStruct((6 * POINTS,...  12 us
    gather x3, local copies, waits for them, and re-layouts, shards(): jnp.take(products, codes.reshape(-1), axis=1).reshape(6 * TILES, LANES)  11.5 us
    all_to_all x2, starting transfers between devices, exchange(): lax.all_to_all(blocks, 'rve', split_axis=0, concat_axis=0, tiled=True)  10 us
    ppermute x2, starting transfers between devices, from_behind(): lax.ppermute(value, axis, [(source, source + steps) for source in range(i...  9.74 us
    pallas_call x1, Pallas kernels, relax(): pl.pallas_call(relax_kernel, out_shape=jax.ShapeDtypeStruct(held.shape, j...  8.37 us
    pallas_call x1, Pallas kernels, hand_over(): pl.pallas_call(kernel, out_shape=jax.ShapeDtypeStruct(slots.shape, slots....  6.58 us
  transfers between devices with their start and end apart: 4, of which 3 were waited for; matrix products, arithmetic and copies ran while one was open for 11% of the time, Pallas kernels for 12%

profile of v2, /device:TPU:24, one launch (start us, length us, event | category | flops | bytes accessed | tf_op | source)
XLA Modules:
  0.0 143.8 jit_solution(5890635866540918436)
XLA Ops:
  0.6 0.7 pad_maximum_fusion.2
  1.4 7.7 %collective-permute-start = (f32[6,1,8,16]{3,2,0,1:T(8,128)S(1)}, f32[6,1,8,16]{3,2,0,1:T(8,128)S(1)}, u32[]{:S(2)}, u32[]{:S(2)}) collective-permute-start(f32[6,1,8,16]{3,2,0,1:T(8,128)S(1)} %pad_maximum_fusion.2), channel_id=1, source_target_pairs={{1,0},{2,1},{3,2},{4,3},{5,4},{6,5},{7,6},{8,7},{9,8},{10,9},{11,1... | collective-permute-start | bytes 9224 | tf_op jit(solution)/shard_map/ppermute | solution.py:31
  9.2 5.0 %all-to-all-start = ((f32[32,256,128]{2,1,0:T(8,128)}), f32[32,256,128]{2,1,0:T(8,128)}, u32[]{:S(2)}, u32[]{:S(2)}) async-start(f32[32,256,128]{2,1,0:T(8,128)} %bitcast.319), calls=%async_computation | async-start | bytes 8388608 | tf_op jit(solution)/shard_map/all_to_all | solution.py:315
  14.3 0.1 compare_and_fusion
  14.4 0.1 minimum_divide_fusion
  14.5 0.1 reshape.1363
  14.6 5.6 %plan.1.plan_ref = s32[512]{0:T(512)} custom-call(s32[128]{0:T(128)} %bitcast.346, s32[128]{0:T(128)} %bitcast.347, s32[128]{0:T(128)} %steps_ref.1), custom_call_target="tpu_custom_call" | custom-call | tf_op jit(solution)/shard_map/plan/pallas_call | solution.py:178
  20.2 0.1 slice.702
  20.3 0.1 slice.685
  20.4 0.1 maximum_subtract_fusion.2
  20.5 0.1 maximum_subtract_fusion.1
  20.6 0.1 slice.675
  20.7 0.1 slice.692
  20.8 0.1 slice.700
  20.9 0.1 fusion.72
  20.9 0.1 fusion.71
  21.0 0.1 slice_maximum_fusion.3
  21.1 0.1 slice_maximum_fusion.2
  21.2 0.1 fusion.64
  21.2 0.1 fusion.56
  21.4 0.1 stack.58
  21.4 0.1 slice.683
  21.5 0.1 fusion.58
  21.6 0.1 stack.53
  21.7 0.1 fusion.92
  21.9 1.0 convolution_multiply_fusion
  22.9 44.8 %all-to-all-done.held_ref = f32[32,256,128]{2,1,0:T(8,128)} async-done(((f32[32,256,128]{2,1,0:T(8,128)}), f32[32,256,128]{2,1,0:T(8,128)}, u32[]{:S(2)}, u32[]{:S(2)}) %all-to-all-start) | async-done | bytes 4194336 | tf_op jit(solution)/shard_map/all_to_all | solution.py:315
  67.7 0.7 copy-done.2
  68.4 8.4 %relax.1.sent_ref = f32[32,256,128]{2,1,0:T(8,128)S(1)} custom-call(s32[512]{0:T(512)S(1)} %copy-done.2, s32[32,128]{1,0:T(8,128)S(1)} %get-tuple-element.120.codes_ref, f32[32,128]{1,0:T(8,128)S(1)} %bitcast.317, f32[32,128]{1,0:T(8,128)S(1)} %bitcast.318, f32[1024,128]{1,0:T(8,128)S(1)} %bitcast.316, f32[32,256,128]{2,1,0:T(8,128)} %all-to-all-done.held_ref), custom_call_target="tpu_custom_call" | custom-call | tf_op jit(solution)/shard_map/relax/pallas_call | solution.py:236
  76.8 2.0 %copy-done = f32[32,256,128]{2,1,0:T(8,128)} copy-done((f32[32,256,128]{2,1,0:T(8,128)}, f32[32,256,128]{2,1,0:T(8,128)S(1)}, u32[]{:S(2)}) %copy-start) | copy-done | bytes 4194328
  78.8 5.0 %all-to-all-start.1 = ((f32[32,256,128]{2,1,0:T(8,128)}), f32[32,256,128]{2,1,0:T(8,128)}, u32[]{:S(2)}, u32[]{:S(2)}) async-start(f32[32,256,128]{2,1,0:T(8,128)} %copy-done), calls=%async_computation.1 | async-start | bytes 8388608 | tf_op jit(solution)/shard_map/all_to_all | solution.py:315
  83.8 0.7 compare_select_fusion
  84.6 10.8 %gather_fusion = f32[4096,6]{1,0:T(8,128)S(1)} fusion(f32[6,128]{0,1:T(8,128)S(1)} %copy-done.6, s32[4096]{0:T(1024)S(1)} %broadcast_clamp_fusion), kind=kCustom, calls=%fused_computation | custom fusion | bytes 212992 | tf_op jit(solution)/shard_map/jit(_take)/gather | solution.py:356
  95.3 0.6 copy.70
  96.1 2.2 %copy-done.1 = f32[32,256,128]{2,1,0:T(8,128)S(1)} copy-done((f32[32,256,128]{2,1,0:T(8,128)S(1)}, f32[32,256,128]{2,1,0:T(8,128)}, u32[]{:S(2)}) %copy-start.1) | copy-done | bytes 4194328
  98.3 12.0 %cell_stress.1 = f32[768,128]{1,0:T(8,128)S(1)} custom-call(s32[512]{0:T(512)S(1)} %copy-done.3, s32[32,128]{1,0:T(8,128)S(1)} %get-tuple-element.120.codes_ref, f32[128,128]{1,0:T(8,128)S(1)} %slice_bitcast_fusion.last_ref, f32[192,128]{1,0:T(8,128)S(1)} %bitcast_select_fusion.basis_ref, f32[32,256,128]{2,1,0:T(8,128)S(1)} %copy-done.1), custom_call_target="tpu_custom_call" | custom-call | tf_op jit(solution)/shard_map/cell_stress/pallas_call | solution.py:278
  110.2 0.2 reduce_sum.9
  110.5 0.1 reshape.1360
  110.7 0.1 slice.735
  110.7 0.1 slice_maximum_fusion
  110.8 0.1 fusion.44
  110.9 2.0 %collective-permute-start.1 = (f32[3,1,8,16]{3,2,0,1:T(8,128)S(1)}, f32[3,1,8,16]{3,2,0,1:T(8,128)S(1)}, u32[]{:S(2)}, u32[]{:S(2)}) collective-permute-start(f32[3,1,8,16]{3,2,0,1:T(8,128)S(1)} %fusion.44), channel_id=1, source_target_pairs={{0,1},{1,2},{2,3},{3,4},{4,5},{5,6},{6,7},{7,8},{8,9},{9,10},{10,1... | collective-permute-start | bytes 4616 | tf_op jit(solution)/shard_map/ppermute | solution.py:31
  112.9 0.1 slice_maximum_fusion.1
  113.0 0.1 slice.727
  113.1 19.3 %collective-permute-done.1 = f32[3,1,8,16]{3,2,0,1:T(8,128)S(1)} collective-permute-done((f32[3,1,8,16]{3,2,0,1:T(8,128)S(1)}, f32[3,1,8,16]{3,2,0,1:T(8,128)S(1)}, u32[]{:S(2)}, u32[]{:S(2)}) %collective-permute-start.1) | collective-permute-done | bytes 1568 | tf_op jit(solution)/shard_map/ppermute | solution.py:31
  132.3 0.7 fusion.50
  133.0 4.3 %all-to-all-done.1 = f32[32,256,128]{2,1,0:T(8,128)} async-done(((f32[32,256,128]{2,1,0:T(8,128)}), f32[32,256,128]{2,1,0:T(8,128)}, u32[]{:S(2)}, u32[]{:S(2)}) %all-to-all-start.1) | async-done | bytes 4194336 | tf_op jit(solution)/shard_map/all_to_all | solution.py:315
  137.3 6.6 %hand_over.1 = f32[256,4096]{1,0:T(8,128)} custom-call(f32[256,4096]{1,0:T(8,128)} %bitcast.48.received_ref), custom_call_target="tpu_custom_call" | custom-call | tf_op jit(solution)/shard_map/hand_over/pallas_call | solution.py:294
  (70 shorter events, 0.5 us)
Async XLA Ops:
  1.4 18.8 %collective-permute-start = (f32[6,1,8,16]{3,2,0,1:T(8,128)S(1)}, f32[6,1,8,16]{3,2,0,1:T(8,128)S(1)}, u32[]{:S(2)}, u32[]{:S(2)}) collective-permute-start(f32[6,1,8,16]{3,2,0,1:T(8,128)S(1)} %pad_maximum_fusion.2), channel_id=1, source_target_pairs={{1,0},{2,1},{3,2},{4,3},{5,4},{6,5},{7,6},{8,7},{9,8},{10,9},{11,1... | collective-permute-start | bytes 9224 | tf_op jit(solution)/shard_map/ppermute | solution.py:31
  9.1 5.1 %copy-start.7 = (s32[2,4096]{1,0:T(2,128)S(1)}, s32[2,4096]{1,0:T(2,128)}, u32[]{:S(2)}) copy-start(s32[2,4096]{1,0:T(2,128)} %param.36) | copy-start | bytes 98308
  9.1 5.1 %copy-start.12 = (s32[128]{0:T(128)S(1)}, s32[128]{0:T(128)}, u32[]{:S(2)}) copy-start(s32[128]{0:T(128)} %steps_ref.1) | copy-start | bytes 1540
  9.1 11.0 %copy-start.8 = (f32[3,1,8,16]{3,2,1,0:T(8,128)S(1)}, f32[3,1,8,16]{3,2,1,0:T(8,128)}, u32[]{:S(2)}) copy-start(f32[3,1,8,16]{3,2,1,0:T(8,128)} %param.32) | copy-start | bytes 4612
  9.2 11.0 %copy-start.9 = (f32[3,1,8,16]{3,2,1,0:T(8,128)S(1)}, f32[3,1,8,16]{3,2,1,0:T(8,128)}, u32[]{:S(2)}) copy-start(f32[3,1,8,16]{3,2,1,0:T(8,128)} %param.31) | copy-start | bytes 4612
  9.2 12.7 %copy-start.11 = (f32[6,128,1]{1,0,2:T(8,128)S(1)}, f32[6,128,1]{1,0,2:T(8,128)}, u32[]{:S(2)}) copy-start(f32[6,128,1]{1,0,2:T(8,128)} %constant.426) | copy-start | bytes 9220
  9.2 58.5 %copy-start.4 = (f32[4096]{0:T(1024)S(1)}, f32[4096]{0:T(1024)}, u32[]{:S(2)}) copy-start(f32[4096]{0:T(1024)} %param.37) | copy-start | bytes 49156
  9.2 58.5 %copy-start.5 = (f32[4096]{0:T(1024)S(1)}, f32[4096]{0:T(1024)}, u32[]{:S(2)}) copy-start(f32[4096]{0:T(1024)} %param.38) | copy-start | bytes 49156
  9.2 58.5 %all-to-all-start = ((f32[32,256,128]{2,1,0:T(8,128)}), f32[32,256,128]{2,1,0:T(8,128)}, u32[]{:S(2)}, u32[]{:S(2)}) async-start(f32[32,256,128]{2,1,0:T(8,128)} %bitcast.319), calls=%async_computation | async-start | bytes 8388608 | tf_op jit(solution)/shard_map/all_to_all | solution.py:315
  20.2 56.6 %copy-start.10 = (f32[3,1,8,16]{3,2,1,0:T(8,128)}, f32[3,1,8,16]{3,2,1,0:T(8,128)S(1)}, u32[]{:S(2)}) copy-start(f32[3,1,8,16]{3,2,1,0:T(8,128)S(1)} %get-tuple-element.135) | copy-start | bytes 4612
  67.7 0.7 copy-start.2
  76.8 2.0 %copy-start = (f32[32,256,128]{2,1,0:T(8,128)}, f32[32,256,128]{2,1,0:T(8,128)S(1)}, u32[]{:S(2)}) copy-start(f32[32,256,128]{2,1,0:T(8,128)S(1)} %relax.1.sent_ref) | copy-start | bytes 12582916
  78.8 5.8 %copy-start.6 = (f32[6,128]{0,1:T(8,128)S(1)}, f32[6,128]{0,1:T(8,128)}, u32[]{:S(2)}) copy-start(f32[6,128]{0,1:T(8,128)} %constant.421.clone) | copy-start | bytes 9220
  78.8 17.3 %copy-start.3 = (s32[512]{0:T(512)S(1)}, s32[512]{0:T(512)}, u32[]{:S(2)}) copy-start(s32[512]{0:T(512)} %plan.1.plan_ref) | copy-start | bytes 6148
  78.8 58.5 %all-to-all-start.1 = ((f32[32,256,128]{2,1,0:T(8,128)}), f32[32,256,128]{2,1,0:T(8,128)}, u32[]{:S(2)}, u32[]{:S(2)}) async-start(f32[32,256,128]{2,1,0:T(8,128)} %copy-done), calls=%async_computation.1 | async-start | bytes 8388608 | tf_op jit(solution)/shard_map/all_to_all | solution.py:315
  96.1 2.2 %copy-start.1 = (f32[32,256,128]{2,1,0:T(8,128)S(1)}, f32[32,256,128]{2,1,0:T(8,128)}, u32[]{:S(2)}) copy-start(f32[32,256,128]{2,1,0:T(8,128)} %copy-done) | copy-start | bytes 12582916
  110.9 21.4 %collective-permute-start.1 = (f32[3,1,8,16]{3,2,0,1:T(8,128)S(1)}, f32[3,1,8,16]{3,2,0,1:T(8,128)S(1)}, u32[]{:S(2)}, u32[]{:S(2)}) collective-permute-start(f32[3,1,8,16]{3,2,0,1:T(8,128)S(1)} %fusion.44), channel_id=1, source_target_pairs={{0,1},{1,2},{2,3},{3,4},{4,5},{5,6},{6,7},{7,8},{8,9},{9,10},{10,1... | collective-permute-start | bytes 4616 | tf_op jit(solution)/shard_map/ppermute | solution.py:31

commit v3 on v2

--- a/solution.py
+++ b/solution.py
@@ -18,6 +18,8 @@
 CAP = 8
 GROUP = 8
 SPAN = 2
+LISTED = 192
+VMEM_LIMIT = 60 * 2**20
 
 young = 10.0
 harden = 1.0
@@ -152,8 +154,8 @@
     for steps in range(NSUB + 1):
         held = seen_ref[2 * OWNERS + steps]
         seen_ref[2 * OWNERS + steps] = start
-        plan_ref[3 * POINTS + steps] = start + held
-        start = start + held
+        start = start + (held + GROUP - 1) // GROUP * GROUP
+        plan_ref[3 * LISTED + steps] = start
 
     def place(element, carry):
         old = old_ref[element]
@@ -166,18 +168,27 @@
         position = seen_ref[level]
         seen_ref[level] = position + 1
         plan_ref[position] = element
-        plan_ref[POINTS + position] = old * CAP + old_rank
-        plan_ref[2 * POINTS + position] = (new - OWNERS) * CAP + new_rank
+        plan_ref[LISTED + position] = old * (TILES * CAP) + old_rank
+        plan_ref[2 * LISTED + position] = (new - OWNERS) * (TILES * CAP) + new_rank
         return carry
 
     lax.fori_loop(0, POINTS, place, 0)
+    for steps in range(1, NSUB + 1):
+        filled = seen_ref[2 * OWNERS + steps]
+
+        def repeat(position, carry, filled=filled):
+            for part in range(3):
+                plan_ref[part * LISTED + position] = plan_ref[part * LISTED + filled - 1]
+            return carry
+
+        lax.fori_loop(filled, plan_ref[3 * LISTED + steps], repeat, 0)
 
 
 def plan(old_owner, new_owner, substeps):
     smem = pl.BlockSpec(memory_space=pltpu.SMEM)
     return pl.pallas_call(
         plan_kernel,
-        out_shape=jax.ShapeDtypeStruct((4 * POINTS,), jnp.int32),
+        out_shape=jax.ShapeDtypeStruct((4 * LISTED,), jnp.int32),
         in_specs=[smem] * 3,
         out_specs=smem,
         scratch_shapes=[pltpu.SMEM((2 * OWNERS + NSUB + 1,), jnp.int32)],
@@ -186,67 +197,110 @@
 
 
 def row_part(row, part):
-    return row >> 3, pl.ds(8 * CAP * part + (row & 7), 8, stride=CAP), slice(None)
-
-
-def relax_kernel(plan_ref, codes_ref, flow_ref, rate_ref, levels_ref, held_ref, sent_ref):
-    sent_ref[...] = jnp.zeros_like(sent_ref)
-    parts = [pl.ds(8 * part, 8) for part in range(SPAN)]
-    for steps in range(1, NSUB + 1):
-        first = plan_ref[3 * POINTS + steps - 1]
-        end = plan_ref[3 * POINTS + steps]
-        gains = []
-        for part in parts:
-            rate = rate_ref[part, :] * ((young + harden) / steps)
-            gains.append(rate / (1.0 + rate))
-
-        def group(turn, carry, steps=steps, first=first, end=end, gains=gains):
-            places = [jnp.minimum(first + GROUP * turn + i, end - 1) for i in range(GROUP)]
-            elements = [plan_ref[place] for place in places]
-            sources = [plan_ref[POINTS + place] for place in places]
-            targets = [plan_ref[2 * POINTS + place] for place in places]
-            state = [
-                [held_ref[row_part(source, part)] * (young + harden) for part in range(SPAN)]
-                for source in sources
-            ]
-            for step in range(steps):
+    return pl.ds(row + 8 * CAP * part, 8, stride=CAP)
+
+
+def relax_kernel(
+    plan_ref,
+    codes_ref,
+    flow_ref,
+    rate_ref,
+    levels_out_ref,
+    held_out_ref,
+    sent_out_ref,
+    levels_ref,
+    held_blocks,
+    sent_blocks,
+    levels_sem,
+    held_sems,
+    sent_sems,
+):
+    held_ref = held_blocks.reshape(OWNERS * TILES * CAP, LANES)
+    sent_ref = sent_blocks.reshape(OWNERS * TILES * CAP, LANES)
+    width = 8 * SPAN * CAP
+    strips = [pl.ds(strip * width, width) for strip in range(TILES // (8 * SPAN))]
+    loads = [
+        pltpu.make_async_copy(held_out_ref.at[:, rows], held_blocks.at[:, rows], held_sems.at[strip])
+        for strip, rows in enumerate(strips)
+    ]
+    stores = [
+        pltpu.make_async_copy(sent_blocks.at[:, rows], sent_out_ref.at[:, rows], sent_sems.at[strip])
+        for strip, rows in enumerate(strips)
+    ]
+    tables = pltpu.make_async_copy(levels_out_ref, levels_ref, levels_sem)
+    loads[0].start()
+    tables.start()
+    for load in loads[1:]:
+        load.start()
+    for strip, rows in enumerate(strips):
+        sent_blocks[:, rows] = jnp.zeros((OWNERS, width, LANES), jnp.float32)
+        if strip == 0:
+            tables.wait()
+        loads[strip].wait()
+        parts = [SPAN * strip + part for part in range(SPAN)]
+        codes = [codes_ref[pl.ds(8 * part, 8), :] for part in parts]
+        flow = [flow_ref[pl.ds(8 * part, 8), :] for part in parts]
+        for steps in range(1, NSUB + 1):
+            first = plan_ref[3 * LISTED + steps - 1]
+            end = plan_ref[3 * LISTED + steps]
+            gains = []
+            for part in parts:
+                rate = rate_ref[pl.ds(8 * part, 8), :] * ((young + harden) / steps)
+                gains.append(rate / (1.0 + rate))
+
+            def group(
+                turn, carry, steps=steps, first=first, gains=gains, parts=parts, codes=codes, flow=flow
+            ):
+                place = first + GROUP * turn
+                elements = [plan_ref[place + i] for i in range(GROUP)]
+                sources = [plan_ref[LISTED + place + i] for i in range(GROUP)]
+                targets = [plan_ref[2 * LISTED + place + i] for i in range(GROUP)]
+                state = [
+                    [held_ref[row_part(source, part), :] * (young + harden) for part in parts]
+                    for source in sources
+                ]
+                for step in range(steps):
+                    for i in range(GROUP):
+                        level = jnp.broadcast_to(
+                            levels_ref[pl.ds(step * POINTS + elements[i], 1), :], (8, LANES)
+                        )
+                        for part in range(SPAN):
+                            stress = jnp.take_along_axis(level, codes[part], axis=1)
+                            trial = stress - state[i][part]
+                            held = jnp.minimum(jnp.maximum(trial, -flow[part]), flow[part])
+                            state[i][part] = state[i][part] + (trial - held) * gains[part]
                 for i in range(GROUP):
-                    level = jnp.broadcast_to(
-                        levels_ref[pl.ds(step * POINTS + elements[i], 1), :], (8, LANES)
-                    )
                     for part in range(SPAN):
-                        stress = jnp.take_along_axis(level, codes_ref[parts[part], :], axis=1)
-                        flow = flow_ref[parts[part], :]
-                        trial = stress - state[i][part]
-                        held = jnp.minimum(jnp.maximum(trial, -flow), flow)
-                        state[i][part] = state[i][part] + (trial - held) * gains[part]
-            for i in range(GROUP):
-                for part in range(SPAN):
-                    sent_ref[row_part(targets[i], part)] = state[i][part] * (
-                        1.0 / (young + harden)
-                    )
-            return carry
-
-        lax.fori_loop(0, (end - first + GROUP - 1) // GROUP, group, 0)
+                        sent_ref[row_part(targets[i], parts[part]), :] = state[i][part] * (
+                            1.0 / (young + harden)
+                        )
+                return carry
+
+            lax.fori_loop(0, (end - first) // GROUP, group, 0)
+        stores[strip].start()
+    for store in stores:
+        store.wait()
 
 
 def relax(order, codes, flow, rate, levels, held):
-    strip = pl.BlockSpec((8 * SPAN, LANES), lambda turn: (turn, 0))
-    rows = pl.BlockSpec((OWNERS, 8 * SPAN * CAP, LANES), lambda turn: (0, turn, 0))
+    smem = pl.BlockSpec(memory_space=pltpu.SMEM)
+    vmem = pl.BlockSpec(memory_space=pltpu.VMEM)
+    outside = pl.BlockSpec(memory_space=pl.ANY)
+    strips = TILES // (8 * SPAN)
     return pl.pallas_call(
         relax_kernel,
         out_shape=jax.ShapeDtypeStruct(held.shape, jnp.float32),
-        grid=(TILES // (8 * SPAN),),
-        in_specs=[
-            pl.BlockSpec(memory_space=pltpu.SMEM),
-            strip,
-            strip,
-            strip,
-            pl.BlockSpec(memory_space=pltpu.VMEM),
-            rows,
+        in_specs=[smem, vmem, vmem, vmem, outside, outside],
+        out_specs=outside,
+        scratch_shapes=[
+            pltpu.VMEM(levels.shape, jnp.float32),
+            pltpu.VMEM(held.shape, jnp.float32),
+            pltpu.VMEM(held.shape, jnp.float32),
+            pltpu.SemaphoreType.DMA,
+            pltpu.SemaphoreType.DMA((strips,)),
+            pltpu.SemaphoreType.DMA((strips,)),
         ],
-        out_specs=rows,
-        compiler_params=pltpu.CompilerParams(vmem_limit_bytes=32 * 2**20),
+        compiler_params=pltpu.CompilerParams(vmem_limit_bytes=VMEM_LIMIT),
         name="relax",
     )(order, codes, flow, rate, levels, held)
 
@@ -254,12 +308,12 @@
 def stress_kernel(plan_ref, codes_ref, last_ref, basis_ref, sent_ref, sums_ref):
     def one(place, carry):
         element = plan_ref[place]
-        target = plan_ref[2 * POINTS + place]
+        target = plan_ref[2 * LISTED + place]
         level = jnp.broadcast_to(last_ref[pl.ds(element, 1), :], (8, LANES))
         totals = [None] * 6
         for quad in range(TILES // 8):
             stress = jnp.take_along_axis(level, codes_ref[pl.ds(8 * quad, 8), :], axis=1)
-            stress = stress - young * sent_ref[row_part(target, quad)]
+            stress = stress - young * sent_ref[row_part(target, quad), :]
             for part in range(6):
                 term = stress * basis_ref[pl.ds(part * TILES + 8 * quad, 8), :]
                 totals[part] = term if quad == 0 else totals[part] + term
@@ -269,7 +323,7 @@
             )
         return carry
 
-    lax.fori_loop(0, POINTS, one, 0)
+    lax.fori_loop(0, plan_ref[3 * LISTED + NSUB], one, 0)
 
 
 def cell_stress(order, codes, last, basis, sent):
@@ -282,21 +336,44 @@
         out_specs=vmem,
         compiler_params=pltpu.CompilerParams(vmem_limit_bytes=32 * 2**20),
         name="cell_stress",
-    )(order, codes, last, basis, sent)
+    )(order, codes, last, basis, sent.reshape(OWNERS * TILES * CAP, LANES))
     return jnp.sum(sums, axis=1).reshape(6, POINTS) / STRUTS
 
 
 def hand_over(slots):
-    def kernel(received_ref, result_ref):
-        result_ref[...] = received_ref[...]
-
-    rows = pl.BlockSpec((slots.shape[0] // 8, slots.shape[1]), lambda turn: (turn, 0))
+    pieces = 4
+    height = slots.shape[0] // pieces
+
+    def kernel(received_ref, result_ref, buffer, in_sems, out_sems):
+        loads, stores = [], []
+        for piece in range(pieces):
+            rows = pl.ds(piece * height, height)
+            loads.append(
+                pltpu.make_async_copy(received_ref.at[rows], buffer.at[rows], in_sems.at[piece])
+            )
+            stores.append(
+                pltpu.make_async_copy(buffer.at[rows], result_ref.at[rows], out_sems.at[piece])
+            )
+        for load in loads:
+            load.start()
+        for load, store in zip(loads, stores):
+            load.wait()
+            store.start()
+        for store in stores:
+            store.wait()
+
+    outside = pl.BlockSpec(memory_space=pl.ANY)
     return pl.pallas_call(
         kernel,
         out_shape=jax.ShapeDtypeStruct(slots.shape, slots.dtype),
-        grid=(8,),
-        in_specs=[rows],
-        out_specs=rows,
+        in_specs=[outside],
+        out_specs=outside,
+        scratch_shapes=[
+            pltpu.VMEM(slots.shape, slots.dtype),
+            pltpu.SemaphoreType.DMA((pieces,)),
+            pltpu.SemaphoreType.DMA((pieces,)),
+        ],
+        compiler_params=pltpu.CompilerParams(vmem_limit_bytes=VMEM_LIMIT),
         name="hand_over",
     )(slots)
 

time: 145 us -> 140 us (0.966)
  waiting for transfers between devices: 68.3 us -> 62.8 us
  Pallas kernels: 32.5 us -> 34.9 us
  local copies, waits for them, and re-layouts: 17.4 us -> 15.6 us
    ppermute x2, waiting for transfers between devices: 19.3 us -> 14.5 us  [from_behind(): lax.ppermute(value, axis, [(source, source + steps) for source in range(i...]
    pallas_call x1, Pallas kernels: 6.58 us -> 3.3 us  [hand_over(): pl.pallas_call(kernel, out_shape=jax.ShapeDtypeStruct(slots.shape, slots....]
    pallas_call x1, Pallas kernels: 12 us -> 14.9 us  [cell_stress(): pl.pallas_call(stress_kernel, out_shape=jax.ShapeDtypeStruct((6 * POINTS,...]
    unnamed x26 -> x20, local copies, waits for them, and re-layouts: 4.93 us -> 2.24 us
    pallas_call x1, Pallas kernels: 8.37 us -> 10.7 us  [relax(): pl.pallas_call(relax_kernel, out_shape=jax.ShapeDtypeStruct(held.shape, j...]
  transfers between devices with their start and end apart: 4 -> 4, of which waited for: 3 -> 3; matrix products, arithmetic and copies ran while one was open for 11% -> 13% of each run, Pallas kernels for 12% -> 15%
where the time goes in v3:
time: 140 us
  waiting for transfers between devices  62.8 us (45%)
  Pallas kernels  34.9 us (25%)
  starting transfers between devices  19.7 us (14%)
  local copies, waits for them, and re-layouts  15.6 us (11%)
  other arithmetic  4.3 us (3%)
  matrix products  1.8 us (1%)
    all_to_all x2, waiting for transfers between devices, exchange(): lax.all_to_all(blocks, 'rve', split_axis=0, concat_axis=0, tiled=True)  48.3 us
    pallas_call x1, Pallas kernels, cell_stress(): pl.pallas_call(stress_kernel, out_shape=jax.ShapeDtypeStruct((6 * POINTS,...  14.9 us
    ppermute x2, waiting for transfers between devices, from_behind(): lax.ppermute(value, axis, [(source, source + steps) for source in range(i...  14.5 us
    gather x3, local copies, waits for them, and re-layouts, shards(): jnp.take(products, codes.reshape(-1), axis=1).reshape(6 * TILES, LANES)  11.5 us
    pallas_call x1, Pallas kernels, relax(): pl.pallas_call(relax_kernel, out_shape=jax.ShapeDtypeStruct(held.shape, j...  10.7 us
    all_to_all x2, starting transfers between devices, exchange(): lax.all_to_all(blocks, 'rve', split_axis=0, concat_axis=0, tiled=True)  10 us
    ppermute x2, starting transfers between devices, from_behind(): lax.ppermute(value, axis, [(source, source + steps) for source in range(i...  9.66 us
    pallas_call x1, Pallas kernels, plan(): pl.pallas_call(plan_kernel, out_shape=jax.ShapeDtypeStruct((4 * LISTED,),...  6.04 us
  transfers between devices with their start and end apart: 4, of which 3 were waited for; matrix products, arithmetic and copies ran while one was open for 13% of the time, Pallas kernels for 15%

profile of v3, /device:TPU:24, one launch (start us, length us, event | category | flops | bytes accessed | tf_op | source)
XLA Modules:
  0.0 140.1 jit_solution(15673768946715957180)
XLA Ops:
  0.6 0.7 pad_maximum_fusion.2
  1.4 7.7 %collective-permute-start = (f32[6,1,8,16]{3,2,0,1:T(8,128)S(1)}, f32[6,1,8,16]{3,2,0,1:T(8,128)S(1)}, u32[]{:S(2)}, u32[]{:S(2)}) collective-permute-start(f32[6,1,8,16]{3,2,0,1:T(8,128)S(1)} %pad_maximum_fusion.2), channel_id=1, source_target_pairs={{1,0},{2,1},{3,2},{4,3},{5,4},{6,5},{7,6},{8,7},{9,8},{10,9},{11,1... | collective-permute-start | bytes 9224 | tf_op jit(solution)/shard_map/ppermute | solution.py:33
  9.2 5.0 %all-to-all-start = ((f32[32,256,128]{2,1,0:T(8,128)}), f32[32,256,128]{2,1,0:T(8,128)}, u32[]{:S(2)}, u32[]{:S(2)}) async-start(f32[32,256,128]{2,1,0:T(8,128)} %bitcast.318), calls=%async_computation | async-start | bytes 8388608 | tf_op jit(solution)/shard_map/all_to_all | solution.py:392
  14.3 0.7 compare_and_fusion
  15.0 0.1 minimum_divide_fusion
  15.0 0.1 reshape.1367
  15.1 6.0 %plan.1.plan_ref = s32[768]{0:T(1024)} custom-call(s32[128]{0:T(128)} %bitcast.348, s32[128]{0:T(128)} %bitcast.349, s32[128]{0:T(128)} %steps_ref.1), custom_call_target="tpu_custom_call" | custom-call | tf_op jit(solution)/shard_map/plan/pallas_call | solution.py:189
  21.3 0.1 slice.702
  21.3 0.1 slice.685
  21.4 0.1 maximum_subtract_fusion.2
  21.5 0.1 maximum_subtract_fusion.1
  21.6 0.1 slice.675
  21.7 0.1 slice.692
  21.8 0.1 slice.700
  21.9 0.1 fusion.72
  21.9 0.1 fusion.71
  22.0 0.1 slice_maximum_fusion.3
  22.1 0.1 slice_maximum_fusion.2
  22.2 0.1 fusion.64
  22.3 0.1 fusion.56
  22.4 0.1 stack.58
  22.5 0.1 slice.683
  22.6 0.1 fusion.58
  22.7 0.1 stack.53
  22.7 0.1 fusion.92
  22.9 1.8 %convolution_multiply_fusion = f32[8,128,128]{2,1,0:T(8,128)} fusion(f32[6,128,1]{1,0,2:T(8,128)S(1)} %copy-done.8, f32[6,8,128]{2,1,0:T(8,128)S(1)} %broadcast_multiply_fusion), kind=kOutput, calls=%fused_computation.1 | convolution fusion | flops 9568256 | bytes 551936 | tf_op jit(solution)/shard_map/cje,cd->jed/dot_general | solution.py:424
  24.7 42.9 %all-to-all-done.held_out_ref = f32[32,256,128]{2,1,0:T(8,128)} async-done(((f32[32,256,128]{2,1,0:T(8,128)}), f32[32,256,128]{2,1,0:T(8,128)}, u32[]{:S(2)}, u32[]{:S(2)}) %all-to-all-start) | async-done | bytes 4194336 | tf_op jit(solution)/shard_map/all_to_all | solution.py:392
  67.7 10.7 %relax.1 = f32[32,256,128]{2,1,0:T(8,128)} custom-call(s32[768]{0:T(1024)} %plan.1.plan_ref, s32[32,128]{1,0:T(8,128)} %get-tuple-element.120.codes_ref, f32[32,128]{1,0:T(8,128)} %bitcast.346, f32[32,128]{1,0:T(8,128)} %bitcast.347, f32[1024,128]{1,0:T(8,128)} %bitcast.319, f32[32,256,128]{2,1,0:T(8,128)} %all-to-all-done.held_out_ref), custom_call_target="tpu_custom_call" | custom-call | tf_op jit(solution)/shard_map/relax/pallas_call | solution.py:290
  78.4 5.0 %all-to-all-start.1 = ((f32[32,256,128]{2,1,0:T(8,128)}), f32[32,256,128]{2,1,0:T(8,128)}, u32[]{:S(2)}, u32[]{:S(2)}) async-start(f32[32,256,128]{2,1,0:T(8,128)} %relax.1), calls=%async_computation.1 | async-start | bytes 8388608 | tf_op jit(solution)/shard_map/all_to_all | solution.py:392
  83.4 0.7 compare_select_fusion
  84.1 10.8 %gather_fusion = f32[4096,6]{1,0:T(8,128)S(1)} fusion(f32[6,128]{0,1:T(8,128)S(1)} %copy-done.3, s32[4096]{0:T(1024)S(1)} %broadcast_clamp_fusion), kind=kCustom, calls=%fused_computation | custom fusion | bytes 212992 | tf_op jit(solution)/shard_map/jit(_take)/gather | solution.py:433
  94.9 0.6 copy.70
  95.5 0.1 gather.7
  95.6 0.8 slice_bitcast_fusion.last_ref
  96.5 2.2 %copy-done = f32[32,256,128]{2,1,0:T(8,128)S(1)} copy-done((f32[32,256,128]{2,1,0:T(8,128)S(1)}, f32[32,256,128]{2,1,0:T(8,128)}, u32[]{:S(2)}) %copy-start) | copy-done | bytes 4194328
  98.7 14.9 %cell_stress.1 = f32[768,128]{1,0:T(8,128)S(1)} custom-call(s32[768]{0:T(1024)S(1)} %copy-done.2, s32[32,128]{1,0:T(8,128)S(1)} %copy-done.1, f32[128,128]{1,0:T(8,128)S(1)} %slice_bitcast_fusion.last_ref, f32[192,128]{1,0:T(8,128)S(1)} %bitcast_select_fusion.basis_ref, f32[8192,128]{1,0:T(8,128)S(1)} %bitcast.317), custom_call_target="tpu_custom_call" | custom-call | tf_op jit(solution)/shard_map/cell_stress/pallas_call | solution.py:332
  113.5 0.2 reduce_sum.9
  113.8 0.1 reshape.1364
  113.9 0.1 slice.735
  114.0 0.1 slice_maximum_fusion
  114.1 0.1 fusion.44
  114.2 1.9 %collective-permute-start.1 = (f32[3,1,8,16]{3,2,0,1:T(8,128)S(1)}, f32[3,1,8,16]{3,2,0,1:T(8,128)S(1)}, u32[]{:S(2)}, u32[]{:S(2)}) collective-permute-start(f32[3,1,8,16]{3,2,0,1:T(8,128)S(1)} %fusion.44), channel_id=1, source_target_pairs={{0,1},{1,2},{2,3},{3,4},{4,5},{5,6},{6,7},{7,8},{8,9},{9,10},{10,1... | collective-permute-start | bytes 4616 | tf_op jit(solution)/shard_map/ppermute | solution.py:33
  116.1 0.1 slice_maximum_fusion.1
  116.2 0.1 slice.727
  116.3 14.5 %collective-permute-done.1 = f32[3,1,8,16]{3,2,0,1:T(8,128)S(1)} collective-permute-done((f32[3,1,8,16]{3,2,0,1:T(8,128)S(1)}, f32[3,1,8,16]{3,2,0,1:T(8,128)S(1)}, u32[]{:S(2)}, u32[]{:S(2)}) %collective-permute-start.1) | collective-permute-done | bytes 1568 | tf_op jit(solution)/shard_map/ppermute | solution.py:33
  130.8 0.7 fusion.50
  131.4 5.4 %all-to-all-done.1 = f32[32,256,128]{2,1,0:T(8,128)} async-done(((f32[32,256,128]{2,1,0:T(8,128)}), f32[32,256,128]{2,1,0:T(8,128)}, u32[]{:S(2)}, u32[]{:S(2)}) %all-to-all-start.1) | async-done | bytes 4194336 | tf_op jit(solution)/shard_map/all_to_all | solution.py:392
  136.8 3.3 %hand_over.1 = f32[256,4096]{1,0:T(8,128)} custom-call(f32[256,4096]{1,0:T(8,128)} %bitcast.49.received_ref), custom_call_target="tpu_custom_call" | custom-call | tf_op jit(solution)/shard_map/hand_over/pallas_call | solution.py:366
  (64 shorter events, 0.4 us)
Async XLA Ops:
  1.4 19.8 %collective-permute-start = (f32[6,1,8,16]{3,2,0,1:T(8,128)S(1)}, f32[6,1,8,16]{3,2,0,1:T(8,128)S(1)}, u32[]{:S(2)}, u32[]{:S(2)}) collective-permute-start(f32[6,1,8,16]{3,2,0,1:T(8,128)S(1)} %pad_maximum_fusion.2), channel_id=1, source_target_pairs={{1,0},{2,1},{3,2},{4,3},{5,4},{6,5},{7,6},{8,7},{9,8},{10,9},{11,1... | collective-permute-start | bytes 9224 | tf_op jit(solution)/shard_map/ppermute | solution.py:33
  9.1 5.1 %copy-start.4 = (s32[2,4096]{1,0:T(2,128)S(1)}, s32[2,4096]{1,0:T(2,128)}, u32[]{:S(2)}) copy-start(s32[2,4096]{1,0:T(2,128)} %param.36) | copy-start | bytes 98308
  9.1 5.1 %copy-start.9 = (s32[128]{0:T(128)S(1)}, s32[128]{0:T(128)}, u32[]{:S(2)}) copy-start(s32[128]{0:T(128)} %steps_ref.1) | copy-start | bytes 1540
  9.1 12.0 %copy-start.5 = (f32[3,1,8,16]{3,2,1,0:T(8,128)S(1)}, f32[3,1,8,16]{3,2,1,0:T(8,128)}, u32[]{:S(2)}) copy-start(f32[3,1,8,16]{3,2,1,0:T(8,128)} %param.32) | copy-start | bytes 4612
  9.2 12.0 %copy-start.6 = (f32[3,1,8,16]{3,2,1,0:T(8,128)S(1)}, f32[3,1,8,16]{3,2,1,0:T(8,128)}, u32[]{:S(2)}) copy-start(f32[3,1,8,16]{3,2,1,0:T(8,128)} %param.31) | copy-start | bytes 4612
  9.2 13.8 %copy-start.8 = (f32[6,128,1]{1,0,2:T(8,128)S(1)}, f32[6,128,1]{1,0,2:T(8,128)}, u32[]{:S(2)}) copy-start(f32[6,128,1]{1,0,2:T(8,128)} %constant.426) | copy-start | bytes 9220
  9.2 58.5 %all-to-all-start = ((f32[32,256,128]{2,1,0:T(8,128)}), f32[32,256,128]{2,1,0:T(8,128)}, u32[]{:S(2)}, u32[]{:S(2)}) async-start(f32[32,256,128]{2,1,0:T(8,128)} %bitcast.318), calls=%async_computation | async-start | bytes 8388608 | tf_op jit(solution)/shard_map/all_to_all | solution.py:392
  21.2 57.1 %copy-start.7 = (f32[3,1,8,16]{3,2,1,0:T(8,128)}, f32[3,1,8,16]{3,2,1,0:T(8,128)S(1)}, u32[]{:S(2)}) copy-start(f32[3,1,8,16]{3,2,1,0:T(8,128)S(1)} %get-tuple-element.135) | copy-start | bytes 4612
  78.3 5.8 %copy-start.3 = (f32[6,128]{0,1:T(8,128)S(1)}, f32[6,128]{0,1:T(8,128)}, u32[]{:S(2)}) copy-start(f32[6,128]{0,1:T(8,128)} %constant.421.clone) | copy-start | bytes 9220
  78.3 18.1 %copy-start.1 = (s32[32,128]{1,0:T(8,128)S(1)}, s32[32,128]{1,0:T(8,128)}, u32[]{:S(2)}) copy-start(s32[32,128]{1,0:T(8,128)} %get-tuple-element.120.codes_ref) | copy-start | bytes 49156
  78.4 18.1 %copy-start.2 = (s32[768]{0:T(1024)S(1)}, s32[768]{0:T(1024)}, u32[]{:S(2)}) copy-start(s32[768]{0:T(1024)} %plan.1.plan_ref) | copy-start | bytes 9220
  78.4 58.5 %all-to-all-start.1 = ((f32[32,256,128]{2,1,0:T(8,128)}), f32[32,256,128]{2,1,0:T(8,128)}, u32[]{:S(2)}, u32[]{:S(2)}) async-start(f32[32,256,128]{2,1,0:T(8,128)} %relax.1), calls=%async_computation.1 | async-start | bytes 8388608 | tf_op jit(solution)/shard_map/all_to_all | solution.py:392
  96.5 2.2 %copy-start = (f32[32,256,128]{2,1,0:T(8,128)S(1)}, f32[32,256,128]{2,1,0:T(8,128)}, u32[]{:S(2)}) copy-start(f32[32,256,128]{2,1,0:T(8,128)} %relax.1) | copy-start | bytes 12582916
  114.2 16.6 %collective-permute-start.1 = (f32[3,1,8,16]{3,2,0,1:T(8,128)S(1)}, f32[3,1,8,16]{3,2,0,1:T(8,128)S(1)}, u32[]{:S(2)}, u32[]{:S(2)}) collective-permute-start(f32[3,1,8,16]{3,2,0,1:T(8,128)S(1)} %fusion.44), channel_id=1, source_target_pairs={{0,1},{1,2},{2,3},{3,4},{4,5},{5,6},{6,7},{7,8},{8,9},{9,10},{10,1... | collective-permute-start | bytes 4616 | tf_op jit(solution)/shard_map/ppermute | solution.py:33

commit v4 on v3

--- a/solution.py
+++ b/solution.py
@@ -14,6 +14,7 @@
 LANES = 128
 POINTS = 128
 TILES = STRUTS // LANES
+EZ = 16
 OWNERS = 32
 CAP = 8
 GROUP = 8
@@ -45,6 +46,22 @@
     return table
 
 
+def table_matrix():
+    steps_of = np.zeros((6, LANES), np.float32)
+    scale = np.zeros((1, LANES), np.float32)
+    for code in range(27):
+        x, y, z = (code // 9 - 1, code // 3 % 3 - 1, code % 3 - 1)
+        length = x * x + y * y + z * z
+        if length == 0:
+            continue
+        steps_of[:, code] = [x * x, y * y, z * z, 2 * x * y, 2 * x * z, 2 * y * z]
+        scale[0, code] = young / length
+    matrix = np.zeros((3, 6, NSUB, NSUB, LANES), np.float32)
+    for step in range(NSUB):
+        matrix[:, :, step, step] = steps_of
+    return matrix.reshape(3 * 6 * NSUB, NSUB * LANES), np.tile(scale, (1, NSUB))
+
+
 def direction_codes(strut_ends):
     first, second = strut_ends[0], strut_ends[1]
 
@@ -56,7 +73,7 @@
     return code.reshape(TILES, LANES)
 
 
-def green(deform):
+def green(deform, stacked=True):
 
     def column_dot(col_a, col_b):
         return (
@@ -65,16 +82,15 @@
             + deform[6 + col_a] * deform[6 + col_b]
         )
 
-    return 0.5 * jnp.stack(
-        [
-            column_dot(0, 0) - 1.0,
-            column_dot(1, 1) - 1.0,
-            column_dot(2, 2) - 1.0,
-            column_dot(0, 1),
-            column_dot(0, 2),
-            column_dot(1, 2),
-        ]
-    )
+    strain = [
+        0.5 * (column_dot(0, 0) - 1.0),
+        0.5 * (column_dot(1, 1) - 1.0),
+        0.5 * (column_dot(2, 2) - 1.0),
+        0.5 * column_dot(0, 1),
+        0.5 * column_dot(0, 2),
+        0.5 * column_dot(1, 2),
+    ]
+    return jnp.stack(strain) if stacked else strain
 
 
 def first_stress(deform, stress):
@@ -137,7 +153,9 @@
     return nodal
 
 
-def plan_kernel(old_ref, new_ref, steps_ref, plan_ref, seen_ref):
+def plan_kernel(old_ref, new_ref, steps_ref, planes_ref, plan_ref, handed_ref, seen_ref):
+    handed_ref[...] = planes_ref[...]
+
     def clear(index, carry):
         seen_ref[index] = 0
         return carry
@@ -184,34 +202,86 @@
         lax.fori_loop(filled, plan_ref[3 * LISTED + steps], repeat, 0)
 
 
-def plan(old_owner, new_owner, substeps):
+def plan(old_owner, new_owner, substeps, planes):
     smem = pl.BlockSpec(memory_space=pltpu.SMEM)
+    vmem = pl.BlockSpec(memory_space=pltpu.VMEM)
     return pl.pallas_call(
         plan_kernel,
-        out_shape=jax.ShapeDtypeStruct((4 * LISTED,), jnp.int32),
-        in_specs=[smem] * 3,
-        out_specs=smem,
+        out_shape=(
+            jax.ShapeDtypeStruct((4 * LISTED,), jnp.int32),
+            jax.ShapeDtypeStruct(planes.shape, planes.dtype),
+        ),
+        in_specs=[smem] * 3 + [vmem],
+        out_specs=(smem, vmem),
         scratch_shapes=[pltpu.SMEM((2 * OWNERS + NSUB + 1,), jnp.int32)],
         name="plan",
-    )(old_owner, new_owner, substeps)
+    )(old_owner, new_owner, substeps, planes)
 
 
 def row_part(row, part):
     return pl.ds(row + 8 * CAP * part, 8, stride=CAP)
 
 
+def next_row(values):
+    return pltpu.roll(values, LANES - EZ, 1)
+
+
+def next_col(values):
+    lane = lax.broadcasted_iota(jnp.int32, values.shape, 1)
+    return jnp.where(
+        lane % EZ == EZ - 1, pltpu.roll(values, EZ - 1, 1), pltpu.roll(values, LANES - 1, 1)
+    )
+
+
+def strain_tables(low, high, fraction, matrix, scale):
+    rise = high - low
+    middle = 0.5 * (low + high)
+    rise = rise + next_col(rise)
+    along_row = next_row(middle) - middle
+    along_col = next_col(middle) - middle
+    slopes = [
+        0.25 * (rise + next_row(rise)),
+        0.5 * (along_row + next_col(along_row)),
+        0.5 * (along_col + next_row(along_col)),
+    ]
+    path = []
+    for row in range(3):
+        for col in range(3):
+            unit = 1.0 if row == col else 0.0
+            old = slopes[col][row : row + 1] + unit
+            new = slopes[col][3 + row : 4 + row] + unit
+            path.append(
+                jnp.broadcast_to(old, (NSUB, LANES))
+                + fraction * jnp.broadcast_to(new - old, (NSUB, LANES))
+            )
+    strain = green(path, False)
+    addends = []
+    for _ in range(3):
+        rounded = [part.astype(jnp.bfloat16).astype(jnp.float32) for part in strain]
+        strain = [part - near for part, near in zip(strain, rounded)]
+        addends += rounded
+    addends = jnp.concatenate(addends, axis=0).astype(jnp.bfloat16)
+    table = lax.dot_general(
+        addends, matrix, (((0,), (0,)), ((), ())), preferred_element_type=jnp.float32
+    )
+    return table * scale
+
+
 def relax_kernel(
     plan_ref,
+    low_ref,
+    high_ref,
+    fraction_ref,
+    matrix_ref,
+    scale_ref,
     codes_ref,
     flow_ref,
     rate_ref,
-    levels_out_ref,
     held_out_ref,
     sent_out_ref,
     levels_ref,
     held_blocks,
     sent_blocks,
-    levels_sem,
     held_sems,
     sent_sems,
 ):
@@ -227,19 +297,20 @@
         pltpu.make_async_copy(sent_blocks.at[:, rows], sent_out_ref.at[:, rows], sent_sems.at[strip])
         for strip, rows in enumerate(strips)
     ]
-    tables = pltpu.make_async_copy(levels_out_ref, levels_ref, levels_sem)
-    loads[0].start()
-    tables.start()
-    for load in loads[1:]:
+    for load in loads:
         load.start()
-    for strip, rows in enumerate(strips):
-        sent_blocks[:, rows] = jnp.zeros((OWNERS, width, LANES), jnp.float32)
-        if strip == 0:
-            tables.wait()
+    table = strain_tables(
+        low_ref[...], high_ref[...], fraction_ref[...], matrix_ref[...], scale_ref[...]
+    )
+    for step in range(NSUB):
+        levels_ref[pl.ds(step * POINTS, POINTS), :] = table[:, step * LANES : (step + 1) * LANES]
+    sent_blocks[...] = jnp.zeros_like(sent_blocks)
+    for strip in range(len(strips)):
         loads[strip].wait()
         parts = [SPAN * strip + part for part in range(SPAN)]
         codes = [codes_ref[pl.ds(8 * part, 8), :] for part in parts]
         flow = [flow_ref[pl.ds(8 * part, 8), :] for part in parts]
+        floor = [-limit for limit in flow]
         for steps in range(1, NSUB + 1):
             first = plan_ref[3 * LISTED + steps - 1]
             end = plan_ref[3 * LISTED + steps]
@@ -248,61 +319,83 @@
                 rate = rate_ref[pl.ds(8 * part, 8), :] * ((young + harden) / steps)
                 gains.append(rate / (1.0 + rate))
 
-            def group(
-                turn, carry, steps=steps, first=first, gains=gains, parts=parts, codes=codes, flow=flow
+            def advance(
+                place, count, steps=steps, gains=gains, parts=parts, codes=codes, flow=flow, floor=floor
             ):
-                place = first + GROUP * turn
-                elements = [plan_ref[place + i] for i in range(GROUP)]
-                sources = [plan_ref[LISTED + place + i] for i in range(GROUP)]
-                targets = [plan_ref[2 * LISTED + place + i] for i in range(GROUP)]
+                elements = [plan_ref[place + i] for i in range(count)]
+                sources = [plan_ref[LISTED + place + i] for i in range(count)]
                 state = [
                     [held_ref[row_part(source, part), :] * (young + harden) for part in parts]
                     for source in sources
                 ]
-                for step in range(steps):
-                    for i in range(GROUP):
-                        level = jnp.broadcast_to(
-                            levels_ref[pl.ds(step * POINTS + elements[i], 1), :], (8, LANES)
-                        )
-                        for part in range(SPAN):
-                            stress = jnp.take_along_axis(level, codes[part], axis=1)
-                            trial = stress - state[i][part]
-                            held = jnp.minimum(jnp.maximum(trial, -flow[part]), flow[part])
-                            state[i][part] = state[i][part] + (trial - held) * gains[part]
-                for i in range(GROUP):
+                for start in range(0, count, GROUP):
+                    for step in range(steps):
+                        for i in range(start, start + GROUP):
+                            level = jnp.broadcast_to(
+                                levels_ref[pl.ds(step * POINTS + elements[i], 1), :],
+                                (8, LANES),
+                            )
+                            for part in range(SPAN):
+                                stress = jnp.take_along_axis(level, codes[part], axis=1)
+                                trial = stress - state[i][part]
+                                held = jnp.minimum(jnp.maximum(trial, floor[part]), flow[part])
+                                state[i][part] = state[i][part] + (trial - held) * gains[part]
+                targets = [plan_ref[2 * LISTED + place + i] for i in range(count)]
+                for i in range(count):
                     for part in range(SPAN):
                         sent_ref[row_part(targets[i], parts[part]), :] = state[i][part] * (
                             1.0 / (young + harden)
                         )
+
+            groups = (end - first) // GROUP
+
+            def pair(turn, carry, first=first, advance=advance):
+                advance(first + 2 * GROUP * turn, 2 * GROUP)
                 return carry
 
-            lax.fori_loop(0, (end - first) // GROUP, group, 0)
+            def single(turn, carry, first=first, advance=advance):
+                advance(first + GROUP * turn, GROUP)
+                return carry
+
+            lax.fori_loop(0, groups // 2, pair, 0)
+            lax.fori_loop(groups // 2 * 2, groups, single, 0)
         stores[strip].start()
     for store in stores:
         store.wait()
 
 
-def relax(order, codes, flow, rate, levels, held):
+def relax(order, low, high, fraction, codes, flow, rate, held):
     smem = pl.BlockSpec(memory_space=pltpu.SMEM)
     vmem = pl.BlockSpec(memory_space=pltpu.VMEM)
     outside = pl.BlockSpec(memory_space=pl.ANY)
     strips = TILES // (8 * SPAN)
+    matrix, scale = table_matrix()
     return pl.pallas_call(
         relax_kernel,
         out_shape=jax.ShapeDtypeStruct(held.shape, jnp.float32),
-        in_specs=[smem, vmem, vmem, vmem, outside, outside],
+        in_specs=[smem] + [vmem] * 8 + [outside],
         out_specs=outside,
         scratch_shapes=[
-            pltpu.VMEM(levels.shape, jnp.float32),
+            pltpu.VMEM((NSUB * POINTS, LANES), jnp.float32),
             pltpu.VMEM(held.shape, jnp.float32),
             pltpu.VMEM(held.shape, jnp.float32),
-            pltpu.SemaphoreType.DMA,
             pltpu.SemaphoreType.DMA((strips,)),
             pltpu.SemaphoreType.DMA((strips,)),
         ],
         compiler_params=pltpu.CompilerParams(vmem_limit_bytes=VMEM_LIMIT),
         name="relax",
-    )(order, codes, flow, rate, levels, held)
+    )(
+        order,
+        low,
+        high,
+        fraction,
+        jnp.asarray(matrix, jnp.bfloat16),
+        jnp.asarray(scale),
+        codes,
+        flow,
+        rate,
+        held,
+    )
 
 
 def stress_kernel(plan_ref, codes_ref, last_ref, basis_ref, sent_ref, sums_ref):
@@ -404,32 +497,28 @@
     plastic_old,
 ):
     planes = displacement.shape[1]
-    both = jnp.concatenate([displacement, velocity], axis=0)
-    rim = from_behind(both, ("macro", "rve"), -1)
     held = exchange(to_tiles(plastic_old))
 
     displacement_next = displacement + time_step * velocity
-    rim_next = rim[:3] + time_step * rim[3:]
-    order = plan(old_owner.reshape(-1), new_owner.reshape(-1), substeps)
+    low = jnp.concatenate([displacement, displacement_next], axis=0).reshape(6, LANES)
+    low = jnp.pad(low, ((0, 2), (0, 0)))
+    order, low = plan(old_owner.reshape(-1), new_owner.reshape(-1), substeps, low)
+    high = from_behind(low, ("macro", "rve"), -1)
     codes = direction_codes(strut_ends)
-    products = jnp.asarray(direction_products())
-    deform_old = element_deform(jnp.concatenate([displacement, rim[:3]], axis=1))
-    deform_new = element_deform(jnp.concatenate([displacement_next, rim_next], axis=1))
     counts = substeps.astype(jnp.float32)
-    change = deform_new - deform_old
-    doubled = jnp.asarray(np.array([1, 1, 1, 2, 2, 2], np.float32))[:, None] * products
     turns = jnp.arange(1, NSUB + 1, dtype=jnp.float32)[:, None]
     fraction = jnp.minimum(turns, counts[None, :]) / counts[None, :]
-    path = deform_old[:, None, :] + fraction[None] * change[:, None, :]
-    levels = young * jnp.einsum("cje,cd->jed", green(path), doubled, precision=highest)
-    last = levels[NSUB - 1]
-    levels = levels.reshape(NSUB * POINTS, LANES)
     flow = flow_stress.reshape(TILES, LANES)
     rate = relax_rate.reshape(TILES, LANES)
-    sent = relax(order, codes, flow, rate, levels, held)
+    sent = relax(order, low, high, fraction, codes, flow, rate, held)
 
     plastic_new = hand_over(from_tiles(exchange(sent)))
 
+    products = jnp.asarray(direction_products())
+    doubled = jnp.asarray(np.array([1, 1, 1, 2, 2, 2], np.float32))[:, None] * products
+    rim_next = high[3:6].reshape(displacement.shape)
+    deform_new = element_deform(jnp.concatenate([displacement_next, rim_next], axis=1))
+    last = young * jnp.einsum("ce,cd->ed", green(deform_new), doubled, precision=highest)
     basis = jnp.take(products, codes.reshape(-1), axis=1).reshape(6 * TILES, LANES)
     stress = cell_stress(order, codes, last, basis, sent)
     piola = first_stress(deform_new, stress)

time: 140 us -> 134 us (0.957)
  waiting for transfers between devices: 62.8 us -> 58.4 us
  starting transfers between devices: 19.7 us -> 22.5 us
  Pallas kernels: 34.9 us -> 32.4 us
  matrix products: 1.8 us -> 0 us
    all_to_all x2, waiting for transfers between devices: 48.3 us -> 14.8 us  [exchange(): lax.all_to_all(blocks, 'rve', split_axis=0, concat_axis=0, tiled=True)]
    ppermute x2, waiting for transfers between devices: 14.5 us -> 43.6 us  [from_behind(): lax.ppermute(value, axis, [(source, source + steps) for source in range(i...]
    all_to_all x2, starting transfers between devices: 10 us -> 13.4 us  [exchange(): lax.all_to_all(blocks, 'rve', split_axis=0, concat_axis=0, tiled=True)]
    dot_general x1 -> x0, matrix products: 1.8 us -> none  [shards(): jnp.einsum('cje,cd->jed', green(path), doubled, precision=highest)]
    pallas_call x1, Pallas kernels: 10.7 us -> 9 us  [relax(): pl.pallas_call(relax_kernel, out_shape=jax.ShapeDtypeStruct(held.shape, j...]
  transfers between devices with their start and end apart: 4 -> 4, of which waited for: 3 -> 4; matrix products, arithmetic and copies ran while one was open for 13% -> 13% of each run, Pallas kernels for 15% -> 15%
where the time goes in v4:
time: 134 us; the launch traced here: 133 us
  waiting for transfers between devices  58.4 us (44%)
  Pallas kernels  32.4 us (24%)
  starting transfers between devices  22.5 us (17%)
  local copies, waits for them, and re-layouts  15.2 us (11%)
  other arithmetic  3.93 us (3%)
    ppermute x2, waiting for transfers between devices, from_behind(): lax.ppermute(value, axis, [(source, source + steps) for source in range(i...  43.6 us
    all_to_all x2, waiting for transfers between devices, exchange(): lax.all_to_all(blocks, 'rve', split_axis=0, concat_axis=0, tiled=True)  14.8 us
    pallas_call x1, Pallas kernels, cell_stress(): pl.pallas_call(stress_kernel, out_shape=jax.ShapeDtypeStruct((6 * POINTS,...  14.1 us
    all_to_all x2, starting transfers between devices, exchange(): lax.all_to_all(blocks, 'rve', split_axis=0, concat_axis=0, tiled=True)  13.4 us
    gather x3, local copies, waits for them, and re-layouts, shards(): jnp.take(products, codes.reshape(-1), axis=1).reshape(6 * TILES, LANES)  11.4 us
    ppermute x2, starting transfers between devices, from_behind(): lax.ppermute(value, axis, [(source, source + steps) for source in range(i...  9.04 us
    pallas_call x1, Pallas kernels, relax(): pl.pallas_call(relax_kernel, out_shape=jax.ShapeDtypeStruct(held.shape, j...  9 us
    pallas_call x1, Pallas kernels, plan(): pl.pallas_call(plan_kernel, out_shape=(jax.ShapeDtypeStruct((4 * LISTED,)...  5.97 us
  transfers between devices with their start and end apart: 4, of which 4 were waited for; matrix products, arithmetic and copies ran while one was open for 13% of the time, Pallas kernels for 15%

profile of v4, /device:TPU:24, one launch (start us, length us, event | category | flops | bytes accessed | tf_op | source)
XLA Modules:
  0.0 133.5 jit_solution(7989302609899627920)
XLA Ops:
  0.7 0.0 copy-start.3
  0.7 8.4 %all-to-all-start = ((f32[32,256,128]{2,1,0:T(8,128)}), f32[32,256,128]{2,1,0:T(8,128)}, u32[]{:S(2)}, u32[]{:S(2)}) async-start(f32[32,256,128]{2,1,0:T(8,128)} %bitcast.291), calls=%async_computation | async-start | bytes 8388608 | tf_op jit(solution)/shard_map/all_to_all | solution.py:485
  9.2 0.0 copy-start.4
  9.2 0.1 reshape.1258
  9.3 0.6 pad.24.planes_ref
  9.9 6.0 %plan.1 = (s32[768]{0:T(1024)}, f32[8,128]{1,0:T(8,128)}) custom-call(s32[128]{0:T(128)} %bitcast.313, s32[128]{0:T(128)} %bitcast.314, s32[128]{0:T(128)} %steps_ref.1, f32[8,128]{1,0:T(8,128)} %pad.24.planes_ref), custom_call_target="tpu_custom_call" | custom-call | tf_op jit(solution)/shard_map/plan/pallas_call | solution.py:208
  15.8 7.1 %collective-permute-start = (f32[8,128]{1,0:T(8,128)}, f32[8,128]{1,0:T(8,128)S(1)}, u32[]{:S(2)}, u32[]{:S(2)}) collective-permute-start(f32[8,128]{1,0:T(8,128)} %get-tuple-element.121.low_ref), channel_id=1, source_target_pairs={{1,0},{2,1},{3,2},{4,3},{5,4},{6,5},{7,6},{8,7},{9,8},{10,9},{11,1... | collective-permute-start | bytes 12296 | tf_op jit(solution)/shard_map/ppermute | solution.py:34
  22.9 0.7 minimum_divide_fusion.fraction_ref
  23.6 0.7 compare_select_fusion
  24.4 0.7 compare_and_fusion
  25.1 0.1 reshape.1268
  25.2 10.8 %gather_fusion = f32[4096,6]{1,0:T(8,128)S(1)} fusion(f32[6,128]{0,1:T(8,128)S(1)} %copy-done.3, s32[4096]{0:T(1024)S(1)} %broadcast_clamp_fusion), kind=kCustom, calls=%fused_computation | custom fusion | bytes 212992 | tf_op jit(solution)/shard_map/jit(_take)/gather | solution.py:522
  36.0 0.6 copy.37
  36.6 0.1 gather.7
  36.7 15.2 %collective-permute-done.high_ref = f32[8,128]{1,0:T(8,128)S(1)} collective-permute-done((f32[8,128]{1,0:T(8,128)}, f32[8,128]{1,0:T(8,128)S(1)}, u32[]{:S(2)}, u32[]{:S(2)}) %collective-permute-start) | collective-permute-done | bytes 4128 | tf_op jit(solution)/shard_map/ppermute | solution.py:34
  51.9 0.1 reshape.1259
  52.0 10.6 %all-to-all-done.held_out_ref = f32[32,256,128]{2,1,0:T(8,128)} async-done(((f32[32,256,128]{2,1,0:T(8,128)}), f32[32,256,128]{2,1,0:T(8,128)}, u32[]{:S(2)}, u32[]{:S(2)}) %all-to-all-start) | async-done | bytes 4194336 | tf_op jit(solution)/shard_map/all_to_all | solution.py:485
  62.6 9.0 %relax.1 = f32[32,256,128]{2,1,0:T(8,128)} custom-call(s32[768]{0:T(1024)} %get-tuple-element.122.plan_ref, f32[8,128]{1,0:T(8,128)} %get-tuple-element.121.low_ref, f32[8,128]{1,0:T(8,128)} %copy-done.8, f32[8,128]{1,0:T(8,128)} %minimum_divide_fusion.fraction_ref, bf16[144,1024]{1,0:T(8,128)(2,1)} %constant.427.clone.matrix_ref, ...), custom_call_target="tpu_custom_call" | custom-call | tf_op jit(solution)/shard_map/relax/pallas_call | solution.py:373
  71.6 0.0 copy-start.9
  71.6 0.0 copy-start.10
  71.6 0.0 copy-start.11
  71.7 0.0 copy-start.13
  71.7 0.0 copy-start.14
  71.7 5.0 %all-to-all-start.1 = ((f32[32,256,128]{2,1,0:T(8,128)}), f32[32,256,128]{2,1,0:T(8,128)}, u32[]{:S(2)}, u32[]{:S(2)}) async-start(f32[32,256,128]{2,1,0:T(8,128)} %relax.1), calls=%async_computation.1 | async-start | bytes 8388608 | tf_op jit(solution)/shard_map/all_to_all | solution.py:485
  76.7 0.1 slice.585
  76.8 0.1 slice.595
  76.9 0.1 maximum_subtract_fusion.1
  77.0 0.1 slice.593
  77.1 0.1 fusion.61
  77.2 0.1 slice_maximum_fusion.2
  77.3 0.1 fusion.54
  77.4 0.1 stack.18
  77.4 0.1 broadcast_add_fusion
  77.6 0.2 fusion.last_ref
  77.8 2.2 %copy-done = f32[32,256,128]{2,1,0:T(8,128)S(1)} copy-done((f32[32,256,128]{2,1,0:T(8,128)S(1)}, f32[32,256,128]{2,1,0:T(8,128)}, u32[]{:S(2)}) %copy-start) | copy-done | bytes 4194328
  80.0 14.1 %cell_stress.1 = f32[768,128]{1,0:T(8,128)S(1)} custom-call(s32[768]{0:T(1024)S(1)} %copy-done.2, s32[32,128]{1,0:T(8,128)S(1)} %copy-done.1, f32[128,128]{1,0:T(8,128)S(1)} %fusion.last_ref, f32[192,128]{1,0:T(8,128)S(1)} %bitcast_select_fusion.basis_ref, f32[8192,128]{1,0:T(8,128)S(1)} %bitcast.290), custom_call_target="tpu_custom_call" | custom-call | tf_op jit(solution)/shard_map/cell_stress/pallas_call | solution.py:425
  94.1 0.2 reduce_sum.9
  94.4 0.1 reshape.1265
  94.6 0.1 slice.619
  94.6 0.1 slice_maximum_fusion
  94.7 0.1 fusion.44
  94.8 2.0 %collective-permute-start.1 = (f32[3,1,8,16]{3,2,0,1:T(8,128)S(1)}, f32[3,1,8,16]{3,2,0,1:T(8,128)S(1)}, u32[]{:S(2)}, u32[]{:S(2)}) collective-permute-start(f32[3,1,8,16]{3,2,0,1:T(8,128)S(1)} %fusion.44), channel_id=1, source_target_pairs={{0,1},{1,2},{2,3},{3,4},{4,5},{5,6},{6,7},{7,8},{8,9},{9,10},{10,1... | collective-permute-start | bytes 4616 | tf_op jit(solution)/shard_map/ppermute | solution.py:34
  96.8 0.1 slice_maximum_fusion.1
  96.9 0.1 slice.611
  97.0 28.4 %collective-permute-done.1 = f32[3,1,8,16]{3,2,0,1:T(8,128)S(1)} collective-permute-done((f32[3,1,8,16]{3,2,0,1:T(8,128)S(1)}, f32[3,1,8,16]{3,2,0,1:T(8,128)S(1)}, u32[]{:S(2)}, u32[]{:S(2)}) %collective-permute-start.1) | collective-permute-done | bytes 1568 | tf_op jit(solution)/shard_map/ppermute | solution.py:34
  125.3 0.7 fusion.50
  126.0 4.2 %all-to-all-done.1 = f32[32,256,128]{2,1,0:T(8,128)} async-done(((f32[32,256,128]{2,1,0:T(8,128)}), f32[32,256,128]{2,1,0:T(8,128)}, u32[]{:S(2)}, u32[]{:S(2)}) %all-to-all-start.1) | async-done | bytes 4194336 | tf_op jit(solution)/shard_map/all_to_all | solution.py:485
  130.2 3.3 %hand_over.1 = f32[256,4096]{1,0:T(8,128)} custom-call(f32[256,4096]{1,0:T(8,128)} %bitcast.40.received_ref), custom_call_target="tpu_custom_call" | custom-call | tf_op jit(solution)/shard_map/hand_over/pallas_call | solution.py:459
  (57 shorter events, 0.3 us)
Async XLA Ops:
  0.6 8.5 %copy-start.6 = (f32[3,1,8,16]{3,2,1,0:T(8,128)S(1)}, f32[3,1,8,16]{3,2,1,0:T(8,128)}, u32[]{:S(2)}) copy-start(f32[3,1,8,16]{3,2,1,0:T(8,128)} %param.34) | copy-start | bytes 4612
  0.6 8.5 %copy-start.7 = (f32[3,1,8,16]{3,2,1,0:T(8,128)S(1)}, f32[3,1,8,16]{3,2,1,0:T(8,128)}, u32[]{:S(2)}) copy-start(f32[3,1,8,16]{3,2,1,0:T(8,128)} %param.33) | copy-start | bytes 4612
  0.7 22.3 %copy-start.15 = (s32[128]{0:T(128)S(1)}, s32[128]{0:T(128)}, u32[]{:S(2)}) copy-start(s32[128]{0:T(128)} %steps_ref.1) | copy-start | bytes 1540
  0.7 23.0 %copy-start.5 = (s32[2,4096]{1,0:T(2,128)S(1)}, s32[2,4096]{1,0:T(2,128)}, u32[]{:S(2)}) copy-start(s32[2,4096]{1,0:T(2,128)} %param.38) | copy-start | bytes 98308
  0.7 24.5 %copy-start.3 = (f32[6,128]{0,1:T(8,128)S(1)}, f32[6,128]{0,1:T(8,128)}, u32[]{:S(2)}) copy-start(f32[6,128]{0,1:T(8,128)} %constant.429.clone) | copy-start | bytes 9220
  0.7 61.9 %all-to-all-start = ((f32[32,256,128]{2,1,0:T(8,128)}), f32[32,256,128]{2,1,0:T(8,128)}, u32[]{:S(2)}, u32[]{:S(2)}) async-start(f32[32,256,128]{2,1,0:T(8,128)} %bitcast.291), calls=%async_computation | async-start | bytes 8388608 | tf_op jit(solution)/shard_map/all_to_all | solution.py:485
  9.2 67.6 %copy-start.4 = (f32[3,1,8,16]{3,2,1,0:T(8,128)}, f32[3,1,8,16]{3,2,1,0:T(8,128)S(1)}, u32[]{:S(2)}) copy-start(f32[3,1,8,16]{3,2,1,0:T(8,128)S(1)} %multiply_add_fusion.5) | copy-start | bytes 4612
  15.8 36.1 %collective-permute-start = (f32[8,128]{1,0:T(8,128)}, f32[8,128]{1,0:T(8,128)S(1)}, u32[]{:S(2)}, u32[]{:S(2)}) collective-permute-start(f32[8,128]{1,0:T(8,128)} %get-tuple-element.121.low_ref), channel_id=1, source_target_pairs={{1,0},{2,1},{3,2},{4,3},{5,4},{6,5},{7,6},{8,7},{9,8},{10,9},{11,1... | collective-permute-start | bytes 12296 | tf_op jit(solution)/shard_map/ppermute | solution.py:34
  51.9 10.7 %copy-start.8 = (f32[8,128]{1,0:T(8,128)}, f32[8,128]{1,0:T(8,128)S(1)}, u32[]{:S(2)}) copy-start(f32[8,128]{1,0:T(8,128)S(1)} %collective-permute-done.high_ref) | copy-start | bytes 12292
  71.6 5.9 %copy-start.9 = (f32[128]{0:T(128)S(1)}, f32[128]{0:T(128)}, u32[]{:S(2)}) copy-start(f32[128]{0:T(128)} %constant.437) | copy-start | bytes 1540
  71.6 5.9 %copy-start.10 = (f32[128]{0:T(128)S(1)}, f32[128]{0:T(128)}, u32[]{:S(2)}) copy-start(f32[128]{0:T(128)} %constant.439) | copy-start | bytes 1540
  71.6 5.9 %copy-start.11 = (f32[128]{0:T(128)S(1)}, f32[128]{0:T(128)}, u32[]{:S(2)}) copy-start(f32[128]{0:T(128)} %constant.441) | copy-start | bytes 1540
  71.6 5.9 %copy-start.12 = (f32[128]{0:T(128)S(1)}, f32[128]{0:T(128)}, u32[]{:S(2)}) copy-start(f32[128]{0:T(128)} %constant.443) | copy-start | bytes 1540
  71.7 5.9 %copy-start.13 = (f32[128]{0:T(128)S(1)}, f32[128]{0:T(128)}, u32[]{:S(2)}) copy-start(f32[128]{0:T(128)} %constant.445) | copy-start | bytes 1540
  71.7 5.9 %copy-start.14 = (f32[128]{0:T(128)S(1)}, f32[128]{0:T(128)}, u32[]{:S(2)}) copy-start(f32[128]{0:T(128)} %constant.447) | copy-start | bytes 1540
  71.7 6.1 %copy-start.1 = (s32[32,128]{1,0:T(8,128)S(1)}, s32[32,128]{1,0:T(8,128)}, u32[]{:S(2)}) copy-start(s32[32,128]{1,0:T(8,128)} %get-tuple-element.124.codes_ref) | copy-start | bytes 49156
  71.7 6.1 %copy-start.2 = (s32[768]{0:T(1024)S(1)}, s32[768]{0:T(1024)}, u32[]{:S(2)}) copy-start(s32[768]{0:T(1024)} %get-tuple-element.122.plan_ref) | copy-start | bytes 9220
  71.7 58.5 %all-to-all-start.1 = ((f32[32,256,128]{2,1,0:T(8,128)}), f32[32,256,128]{2,1,0:T(8,128)}, u32[]{:S(2)}, u32[]{:S(2)}) async-start(f32[32,256,128]{2,1,0:T(8,128)} %relax.1), calls=%async_computation.1 | async-start | bytes 8388608 | tf_op jit(solution)/shard_map/all_to_all | solution.py:485
  77.8 2.2 %copy-start = (f32[32,256,128]{2,1,0:T(8,128)S(1)}, f32[32,256,128]{2,1,0:T(8,128)}, u32[]{:S(2)}) copy-start(f32[32,256,128]{2,1,0:T(8,128)} %relax.1) | copy-start | bytes 12582916
  94.8 30.5 %collective-permute-start.1 = (f32[3,1,8,16]{3,2,0,1:T(8,128)S(1)}, f32[3,1,8,16]{3,2,0,1:T(8,128)S(1)}, u32[]{:S(2)}, u32[]{:S(2)}) collective-permute-start(f32[3,1,8,16]{3,2,0,1:T(8,128)S(1)} %fusion.44), channel_id=1, source_target_pairs={{0,1},{1,2},{2,3},{3,4},{4,5},{5,6},{6,7},{7,8},{8,9},{9,10},{10,1... | collective-permute-start | bytes 4616 | tf_op jit(solution)/shard_map/ppermute | solution.py:34

commit v5 on v4

--- a/solution.py
+++ b/solution.py
@@ -55,7 +55,7 @@
         if length == 0:
             continue
         steps_of[:, code] = [x * x, y * y, z * z, 2 * x * y, 2 * x * z, 2 * y * z]
-        scale[0, code] = young / length
+        scale[0, code] = young / (young + harden) / length
     matrix = np.zeros((3, 6, NSUB, NSUB, LANES), np.float32)
     for step in range(NSUB):
         matrix[:, :, step, step] = steps_of
@@ -309,7 +309,7 @@
         loads[strip].wait()
         parts = [SPAN * strip + part for part in range(SPAN)]
         codes = [codes_ref[pl.ds(8 * part, 8), :] for part in parts]
-        flow = [flow_ref[pl.ds(8 * part, 8), :] for part in parts]
+        flow = [flow_ref[pl.ds(8 * part, 8), :] * (1.0 / (young + harden)) for part in parts]
         floor = [-limit for limit in flow]
         for steps in range(1, NSUB + 1):
             first = plan_ref[3 * LISTED + steps - 1]
@@ -325,12 +325,12 @@
                 elements = [plan_ref[place + i] for i in range(count)]
                 sources = [plan_ref[LISTED + place + i] for i in range(count)]
                 state = [
-                    [held_ref[row_part(source, part), :] * (young + harden) for part in parts]
+                    [held_ref[row_part(source, part), :] for part in parts]
                     for source in sources
                 ]
-                for start in range(0, count, GROUP):
+                for start in range(0, count, 4):
                     for step in range(steps):
-                        for i in range(start, start + GROUP):
+                        for i in range(start, start + 4):
                             level = jnp.broadcast_to(
                                 levels_ref[pl.ds(step * POINTS + elements[i], 1), :],
                                 (8, LANES),
@@ -343,9 +343,7 @@
                 targets = [plan_ref[2 * LISTED + place + i] for i in range(count)]
                 for i in range(count):
                     for part in range(SPAN):
-                        sent_ref[row_part(targets[i], parts[part]), :] = state[i][part] * (
-                            1.0 / (young + harden)
-                        )
+                        sent_ref[row_part(targets[i], parts[part]), :] = state[i][part]
 
             groups = (end - first) // GROUP
 

time: 134 us -> 134 us (level)
  no operation moved by 1% of the time
where the time goes in v5:
time: 134 us; the launch traced here: 133 us
  waiting for transfers between devices  58.4 us (44%)
  Pallas kernels  32.3 us (24%)
  starting transfers between devices  22.4 us (17%)
  local copies, waits for them, and re-layouts  15.2 us (11%)
  other arithmetic  3.93 us (3%)
    ppermute x2, waiting for transfers between devices, from_behind(): lax.ppermute(value, axis, [(source, source + steps) for source in range(i...  43.6 us
    all_to_all x2, waiting for transfers between devices, exchange(): lax.all_to_all(blocks, 'rve', split_axis=0, concat_axis=0, tiled=True)  14.8 us
    pallas_call x1, Pallas kernels, cell_stress(): pl.pallas_call(stress_kernel, out_shape=jax.ShapeDtypeStruct((6 * POINTS,...  14.1 us
    all_to_all x2, starting transfers between devices, exchange(): lax.all_to_all(blocks, 'rve', split_axis=0, concat_axis=0, tiled=True)  13.4 us
    gather x3, local copies, waits for them, and re-layouts, shards(): jnp.take(products, codes.reshape(-1), axis=1).reshape(6 * TILES, LANES)  11.4 us
    ppermute x2, starting transfers between devices, from_behind(): lax.ppermute(value, axis, [(source, source + steps) for source in range(i...  8.96 us
    pallas_call x1, Pallas kernels, relax(): pl.pallas_call(relax_kernel, out_shape=jax.ShapeDtypeStruct(held.shape, j...  8.93 us
    pallas_call x1, Pallas kernels, plan(): pl.pallas_call(plan_kernel, out_shape=(jax.ShapeDtypeStruct((4 * LISTED,)...  5.97 us
  transfers between devices with their start and end apart: 4, of which 4 were waited for; matrix products, arithmetic and copies ran while one was open for 13% of the time, Pallas kernels for 15%

profile of v5, /device:TPU:24, one launch (start us, length us, event | category | flops | bytes accessed | tf_op | source)
XLA Modules:
  0.0 133.4 jit_solution(4727561967857990055)
XLA Ops:
  0.7 0.0 copy-start.3
  0.7 8.4 %all-to-all-start = ((f32[32,256,128]{2,1,0:T(8,128)}), f32[32,256,128]{2,1,0:T(8,128)}, u32[]{:S(2)}, u32[]{:S(2)}) async-start(f32[32,256,128]{2,1,0:T(8,128)} %bitcast.291), calls=%async_computation | async-start | bytes 8388608 | tf_op jit(solution)/shard_map/all_to_all | solution.py:483
  9.2 0.0 copy-start.4
  9.2 0.1 reshape.1258
  9.3 0.6 pad.24.planes_ref
  9.9 6.0 %plan.1 = (s32[768]{0:T(1024)}, f32[8,128]{1,0:T(8,128)}) custom-call(s32[128]{0:T(128)} %bitcast.313, s32[128]{0:T(128)} %bitcast.314, s32[128]{0:T(128)} %steps_ref.1, f32[8,128]{1,0:T(8,128)} %pad.24.planes_ref), custom_call_target="tpu_custom_call" | custom-call | tf_op jit(solution)/shard_map/plan/pallas_call | solution.py:208
  15.8 7.0 %collective-permute-start = (f32[8,128]{1,0:T(8,128)}, f32[8,128]{1,0:T(8,128)S(1)}, u32[]{:S(2)}, u32[]{:S(2)}) collective-permute-start(f32[8,128]{1,0:T(8,128)} %get-tuple-element.121.low_ref), channel_id=1, source_target_pairs={{1,0},{2,1},{3,2},{4,3},{5,4},{6,5},{7,6},{8,7},{9,8},{10,9},{11,1... | collective-permute-start | bytes 12296 | tf_op jit(solution)/shard_map/ppermute | solution.py:34
  22.9 0.7 minimum_divide_fusion.fraction_ref
  23.5 0.7 compare_select_fusion
  24.3 0.7 compare_and_fusion
  25.0 0.1 reshape.1268
  25.1 10.8 %gather_fusion = f32[4096,6]{1,0:T(8,128)S(1)} fusion(f32[6,128]{0,1:T(8,128)S(1)} %copy-done.3, s32[4096]{0:T(1024)S(1)} %broadcast_clamp_fusion), kind=kCustom, calls=%fused_computation | custom fusion | bytes 212992 | tf_op jit(solution)/shard_map/jit(_take)/gather | solution.py:520
  35.9 0.6 copy.37
  36.5 0.1 gather.7
  36.6 15.3 %collective-permute-done.high_ref = f32[8,128]{1,0:T(8,128)S(1)} collective-permute-done((f32[8,128]{1,0:T(8,128)}, f32[8,128]{1,0:T(8,128)S(1)}, u32[]{:S(2)}, u32[]{:S(2)}) %collective-permute-start) | collective-permute-done | bytes 4128 | tf_op jit(solution)/shard_map/ppermute | solution.py:34
  51.9 0.1 reshape.1259
  52.0 10.6 %all-to-all-done.held_out_ref = f32[32,256,128]{2,1,0:T(8,128)} async-done(((f32[32,256,128]{2,1,0:T(8,128)}), f32[32,256,128]{2,1,0:T(8,128)}, u32[]{:S(2)}, u32[]{:S(2)}) %all-to-all-start) | async-done | bytes 4194336 | tf_op jit(solution)/shard_map/all_to_all | solution.py:483
  62.6 8.9 %relax.1 = f32[32,256,128]{2,1,0:T(8,128)} custom-call(s32[768]{0:T(1024)} %get-tuple-element.122.plan_ref, f32[8,128]{1,0:T(8,128)} %get-tuple-element.121.low_ref, f32[8,128]{1,0:T(8,128)} %copy-done.8, f32[8,128]{1,0:T(8,128)} %minimum_divide_fusion.fraction_ref, bf16[144,1024]{1,0:T(8,128)(2,1)} %constant.427.clone.matrix_ref, ...), custom_call_target="tpu_custom_call" | custom-call | tf_op jit(solution)/shard_map/relax/pallas_call | solution.py:371
  71.6 0.0 copy-start.10
  71.6 0.0 copy-start.11
  71.6 0.0 copy-start.12
  71.6 0.0 copy-start.13
  71.6 0.0 copy-start.14
  71.6 5.0 %all-to-all-start.1 = ((f32[32,256,128]{2,1,0:T(8,128)}), f32[32,256,128]{2,1,0:T(8,128)}, u32[]{:S(2)}, u32[]{:S(2)}) async-start(f32[32,256,128]{2,1,0:T(8,128)} %relax.1), calls=%async_computation.1 | async-start | bytes 8388608 | tf_op jit(solution)/shard_map/all_to_all | solution.py:483
  76.7 0.1 slice.585
  76.8 0.1 slice.595
  76.8 0.1 maximum_subtract_fusion.1
  76.9 0.1 slice.593
  77.0 0.1 fusion.61
  77.1 0.1 slice_maximum_fusion.2
  77.2 0.1 fusion.54
  77.3 0.1 stack.18
  77.4 0.1 broadcast_add_fusion
  77.5 0.2 fusion.last_ref
  77.8 2.2 %copy-done = f32[32,256,128]{2,1,0:T(8,128)S(1)} copy-done((f32[32,256,128]{2,1,0:T(8,128)S(1)}, f32[32,256,128]{2,1,0:T(8,128)}, u32[]{:S(2)}) %copy-start) | copy-done | bytes 4194328
  79.9 14.1 %cell_stress.1 = f32[768,128]{1,0:T(8,128)S(1)} custom-call(s32[768]{0:T(1024)S(1)} %copy-done.2, s32[32,128]{1,0:T(8,128)S(1)} %copy-done.1, f32[128,128]{1,0:T(8,128)S(1)} %fusion.last_ref, f32[192,128]{1,0:T(8,128)S(1)} %bitcast_select_fusion.basis_ref, f32[8192,128]{1,0:T(8,128)S(1)} %bitcast.290), custom_call_target="tpu_custom_call" | custom-call | tf_op jit(solution)/shard_map/cell_stress/pallas_call | solution.py:423
  94.1 0.2 reduce_sum.9
  94.4 0.1 reshape.1265
  94.5 0.1 slice.619
  94.6 0.1 slice_maximum_fusion
  94.7 0.1 fusion.44
  94.7 2.0 %collective-permute-start.1 = (f32[3,1,8,16]{3,2,0,1:T(8,128)S(1)}, f32[3,1,8,16]{3,2,0,1:T(8,128)S(1)}, u32[]{:S(2)}, u32[]{:S(2)}) collective-permute-start(f32[3,1,8,16]{3,2,0,1:T(8,128)S(1)} %fusion.44), channel_id=1, source_target_pairs={{0,1},{1,2},{2,3},{3,4},{4,5},{5,6},{6,7},{7,8},{8,9},{9,10},{10,1... | collective-permute-start | bytes 4616 | tf_op jit(solution)/shard_map/ppermute | solution.py:34
  96.7 0.1 slice_maximum_fusion.1
  96.8 0.1 slice.611
  96.9 28.3 %collective-permute-done.1 = f32[3,1,8,16]{3,2,0,1:T(8,128)S(1)} collective-permute-done((f32[3,1,8,16]{3,2,0,1:T(8,128)S(1)}, f32[3,1,8,16]{3,2,0,1:T(8,128)S(1)}, u32[]{:S(2)}, u32[]{:S(2)}) %collective-permute-start.1) | collective-permute-done | bytes 1568 | tf_op jit(solution)/shard_map/ppermute | solution.py:34
  125.2 0.7 fusion.50
  125.9 4.3 %all-to-all-done.1 = f32[32,256,128]{2,1,0:T(8,128)} async-done(((f32[32,256,128]{2,1,0:T(8,128)}), f32[32,256,128]{2,1,0:T(8,128)}, u32[]{:S(2)}, u32[]{:S(2)}) %all-to-all-start.1) | async-done | bytes 4194336 | tf_op jit(solution)/shard_map/all_to_all | solution.py:483
  130.1 3.3 %hand_over.1 = f32[256,4096]{1,0:T(8,128)} custom-call(f32[256,4096]{1,0:T(8,128)} %bitcast.40.received_ref), custom_call_target="tpu_custom_call" | custom-call | tf_op jit(solution)/shard_map/hand_over/pallas_call | solution.py:457
  (57 shorter events, 0.3 us)
Async XLA Ops:
  0.6 8.5 %copy-start.6 = (f32[3,1,8,16]{3,2,1,0:T(8,128)S(1)}, f32[3,1,8,16]{3,2,1,0:T(8,128)}, u32[]{:S(2)}) copy-start(f32[3,1,8,16]{3,2,1,0:T(8,128)} %param.34) | copy-start | bytes 4612
  0.6 8.5 %copy-start.7 = (f32[3,1,8,16]{3,2,1,0:T(8,128)S(1)}, f32[3,1,8,16]{3,2,1,0:T(8,128)}, u32[]{:S(2)}) copy-start(f32[3,1,8,16]{3,2,1,0:T(8,128)} %param.33) | copy-start | bytes 4612
  0.7 22.2 %copy-start.15 = (s32[128]{0:T(128)S(1)}, s32[128]{0:T(128)}, u32[]{:S(2)}) copy-start(s32[128]{0:T(128)} %steps_ref.1) | copy-start | bytes 1540
  0.7 22.9 %copy-start.5 = (s32[2,4096]{1,0:T(2,128)S(1)}, s32[2,4096]{1,0:T(2,128)}, u32[]{:S(2)}) copy-start(s32[2,4096]{1,0:T(2,128)} %param.38) | copy-start | bytes 98308
  0.7 24.4 %copy-start.3 = (f32[6,128]{0,1:T(8,128)S(1)}, f32[6,128]{0,1:T(8,128)}, u32[]{:S(2)}) copy-start(f32[6,128]{0,1:T(8,128)} %constant.429.clone) | copy-start | bytes 9220
  0.7 61.9 %all-to-all-start = ((f32[32,256,128]{2,1,0:T(8,128)}), f32[32,256,128]{2,1,0:T(8,128)}, u32[]{:S(2)}, u32[]{:S(2)}) async-start(f32[32,256,128]{2,1,0:T(8,128)} %bitcast.291), calls=%async_computation | async-start | bytes 8388608 | tf_op jit(solution)/shard_map/all_to_all | solution.py:483
  9.2 67.5 %copy-start.4 = (f32[3,1,8,16]{3,2,1,0:T(8,128)}, f32[3,1,8,16]{3,2,1,0:T(8,128)S(1)}, u32[]{:S(2)}) copy-start(f32[3,1,8,16]{3,2,1,0:T(8,128)S(1)} %multiply_add_fusion.5) | copy-start | bytes 4612
  15.8 36.1 %collective-permute-start = (f32[8,128]{1,0:T(8,128)}, f32[8,128]{1,0:T(8,128)S(1)}, u32[]{:S(2)}, u32[]{:S(2)}) collective-permute-start(f32[8,128]{1,0:T(8,128)} %get-tuple-element.121.low_ref), channel_id=1, source_target_pairs={{1,0},{2,1},{3,2},{4,3},{5,4},{6,5},{7,6},{8,7},{9,8},{10,9},{11,1... | collective-permute-start | bytes 12296 | tf_op jit(solution)/shard_map/ppermute | solution.py:34
  51.9 10.7 %copy-start.8 = (f32[8,128]{1,0:T(8,128)}, f32[8,128]{1,0:T(8,128)S(1)}, u32[]{:S(2)}) copy-start(f32[8,128]{1,0:T(8,128)S(1)} %collective-permute-done.high_ref) | copy-start | bytes 12292
  71.5 5.9 %copy-start.9 = (f32[128]{0:T(128)S(1)}, f32[128]{0:T(128)}, u32[]{:S(2)}) copy-start(f32[128]{0:T(128)} %constant.437) | copy-start | bytes 1540
  71.6 5.9 %copy-start.10 = (f32[128]{0:T(128)S(1)}, f32[128]{0:T(128)}, u32[]{:S(2)}) copy-start(f32[128]{0:T(128)} %constant.439) | copy-start | bytes 1540
  71.6 5.9 %copy-start.11 = (f32[128]{0:T(128)S(1)}, f32[128]{0:T(128)}, u32[]{:S(2)}) copy-start(f32[128]{0:T(128)} %constant.441) | copy-start | bytes 1540
  71.6 5.9 %copy-start.12 = (f32[128]{0:T(128)S(1)}, f32[128]{0:T(128)}, u32[]{:S(2)}) copy-start(f32[128]{0:T(128)} %constant.443) | copy-start | bytes 1540
  71.6 5.9 %copy-start.13 = (f32[128]{0:T(128)S(1)}, f32[128]{0:T(128)}, u32[]{:S(2)}) copy-start(f32[128]{0:T(128)} %constant.445) | copy-start | bytes 1540
  71.6 5.9 %copy-start.14 = (f32[128]{0:T(128)S(1)}, f32[128]{0:T(128)}, u32[]{:S(2)}) copy-start(f32[128]{0:T(128)} %constant.447) | copy-start | bytes 1540
  71.6 6.1 %copy-start.1 = (s32[32,128]{1,0:T(8,128)S(1)}, s32[32,128]{1,0:T(8,128)}, u32[]{:S(2)}) copy-start(s32[32,128]{1,0:T(8,128)} %get-tuple-element.124.codes_ref) | copy-start | bytes 49156
  71.6 6.1 %copy-start.2 = (s32[768]{0:T(1024)S(1)}, s32[768]{0:T(1024)}, u32[]{:S(2)}) copy-start(s32[768]{0:T(1024)} %get-tuple-element.122.plan_ref) | copy-start | bytes 9220
  71.6 58.5 %all-to-all-start.1 = ((f32[32,256,128]{2,1,0:T(8,128)}), f32[32,256,128]{2,1,0:T(8,128)}, u32[]{:S(2)}, u32[]{:S(2)}) async-start(f32[32,256,128]{2,1,0:T(8,128)} %relax.1), calls=%async_computation.1 | async-start | bytes 8388608 | tf_op jit(solution)/shard_map/all_to_all | solution.py:483
  77.7 2.2 %copy-start = (f32[32,256,128]{2,1,0:T(8,128)S(1)}, f32[32,256,128]{2,1,0:T(8,128)}, u32[]{:S(2)}) copy-start(f32[32,256,128]{2,1,0:T(8,128)} %relax.1) | copy-start | bytes 12582916
  94.7 30.4 %collective-permute-start.1 = (f32[3,1,8,16]{3,2,0,1:T(8,128)S(1)}, f32[3,1,8,16]{3,2,0,1:T(8,128)S(1)}, u32[]{:S(2)}, u32[]{:S(2)}) collective-permute-start(f32[3,1,8,16]{3,2,0,1:T(8,128)S(1)} %fusion.44), channel_id=1, source_target_pairs={{0,1},{1,2},{2,3},{3,4},{4,5},{5,6},{6,7},{7,8},{8,9},{9,10},{10,1... | collective-permute-start | bytes 4616 | tf_op jit(solution)/shard_map/ppermute | solution.py:34

commit v6 on v5

--- a/solution.py
+++ b/solution.py
@@ -297,8 +297,7 @@
         pltpu.make_async_copy(sent_blocks.at[:, rows], sent_out_ref.at[:, rows], sent_sems.at[strip])
         for strip, rows in enumerate(strips)
     ]
-    for load in loads:
-        load.start()
+    loads[0].start()
     table = strain_tables(
         low_ref[...], high_ref[...], fraction_ref[...], matrix_ref[...], scale_ref[...]
     )
@@ -307,6 +306,8 @@
     sent_blocks[...] = jnp.zeros_like(sent_blocks)
     for strip in range(len(strips)):
         loads[strip].wait()
+        if strip + 1 < len(strips):
+            loads[strip + 1].start()
         parts = [SPAN * strip + part for part in range(SPAN)]
         codes = [codes_ref[pl.ds(8 * part, 8), :] for part in parts]
         flow = [flow_ref[pl.ds(8 * part, 8), :] * (1.0 / (young + harden)) for part in parts]
@@ -432,13 +433,13 @@
 
 
 def hand_over(slots):
-    pieces = 4
-    height = slots.shape[0] // pieces
+    heights = (16, 48, 64, 64, 48, 16)
+    pieces = len(heights)
 
     def kernel(received_ref, result_ref, buffer, in_sems, out_sems):
         loads, stores = [], []
         for piece in range(pieces):
-            rows = pl.ds(piece * height, height)
+            rows = pl.ds(sum(heights[:piece]), heights[piece])
             loads.append(
                 pltpu.make_async_copy(received_ref.at[rows], buffer.at[rows], in_sems.at[piece])
             )

time: 134 us -> 135 us (level)
  Pallas kernels: 32.3 us -> 33.7 us
  transfers between devices with their start and end apart: 4 -> 4, of which waited for: 4 -> 4; matrix products, arithmetic and copies ran while one was open for 13% -> 13% of each run, Pallas kernels for 15% -> 16%
where the time goes in v6:
time: 135 us; the launch traced here: 134 us
  waiting for transfers between devices  57.7 us (43%)
  Pallas kernels  33.7 us (25%)
  starting transfers between devices  22.4 us (17%)
  local copies, waits for them, and re-layouts  15.2 us (11%)
  other arithmetic  3.93 us (3%)
    ppermute x2, waiting for transfers between devices, from_behind(): lax.ppermute(value, axis, [(source, source + steps) for source in range(i...  43.1 us
    pallas_call x1, Pallas kernels, cell_stress(): pl.pallas_call(stress_kernel, out_shape=jax.ShapeDtypeStruct((6 * POINTS,...  14.9 us
    all_to_all x2, waiting for transfers between devices, exchange(): lax.all_to_all(blocks, 'rve', split_axis=0, concat_axis=0, tiled=True)  14.5 us
    all_to_all x2, starting transfers between devices, exchange(): lax.all_to_all(blocks, 'rve', split_axis=0, concat_axis=0, tiled=True)  13.4 us
    gather x3, local copies, waits for them, and re-layouts, shards(): jnp.take(products, codes.reshape(-1), axis=1).reshape(6 * TILES, LANES)  11.4 us
    pallas_call x1, Pallas kernels, relax(): pl.pallas_call(relax_kernel, out_shape=jax.ShapeDtypeStruct(held.shape, j...  9.43 us
    ppermute x2, starting transfers between devices, from_behind(): lax.ppermute(value, axis, [(source, source + steps) for source in range(i...  8.96 us
    pallas_call x1, Pallas kernels, plan(): pl.pallas_call(plan_kernel, out_shape=(jax.ShapeDtypeStruct((4 * LISTED,)...  6.06 us
  transfers between devices with their start and end apart: 4, of which 4 were waited for; matrix products, arithmetic and copies ran while one was open for 13% of the time, Pallas kernels for 16%

profile of v6, /device:TPU:24, one launch (start us, length us, event | category | flops | bytes accessed | tf_op | source)
XLA Modules:
  0.0 134.0 jit_solution(11231459097492912789)
XLA Ops:
  0.7 0.0 copy-start.3
  0.7 8.4 %all-to-all-start = ((f32[32,256,128]{2,1,0:T(8,128)}), f32[32,256,128]{2,1,0:T(8,128)}, u32[]{:S(2)}, u32[]{:S(2)}) async-start(f32[32,256,128]{2,1,0:T(8,128)} %bitcast.291), calls=%async_computation | async-start | bytes 8388608 | tf_op jit(solution)/shard_map/all_to_all | solution.py:484
  9.2 0.0 copy-start.4
  9.2 0.1 reshape.1258
  9.3 0.6 pad.24.planes_ref
  9.9 6.1 %plan.1 = (s32[768]{0:T(1024)}, f32[8,128]{1,0:T(8,128)}) custom-call(s32[128]{0:T(128)} %bitcast.313, s32[128]{0:T(128)} %bitcast.314, s32[128]{0:T(128)} %steps_ref.1, f32[8,128]{1,0:T(8,128)} %pad.24.planes_ref), custom_call_target="tpu_custom_call" | custom-call | tf_op jit(solution)/shard_map/plan/pallas_call | solution.py:208
  15.9 7.0 %collective-permute-start = (f32[8,128]{1,0:T(8,128)}, f32[8,128]{1,0:T(8,128)S(1)}, u32[]{:S(2)}, u32[]{:S(2)}) collective-permute-start(f32[8,128]{1,0:T(8,128)} %get-tuple-element.121.low_ref), channel_id=1, source_target_pairs={{1,0},{2,1},{3,2},{4,3},{5,4},{6,5},{7,6},{8,7},{9,8},{10,9},{11,1... | collective-permute-start | bytes 12296 | tf_op jit(solution)/shard_map/ppermute | solution.py:34
  22.9 0.7 minimum_divide_fusion.fraction_ref
  23.6 0.7 compare_select_fusion
  24.4 0.7 compare_and_fusion
  25.1 0.1 reshape.1268
  25.2 10.8 %gather_fusion = f32[4096,6]{1,0:T(8,128)S(1)} fusion(f32[6,128]{0,1:T(8,128)S(1)} %copy-done.3, s32[4096]{0:T(1024)S(1)} %broadcast_clamp_fusion), kind=kCustom, calls=%fused_computation | custom fusion | bytes 212992 | tf_op jit(solution)/shard_map/jit(_take)/gather | solution.py:521
  36.0 0.6 copy.37
  36.6 0.1 gather.7
  36.7 15.3 %collective-permute-done.high_ref = f32[8,128]{1,0:T(8,128)S(1)} collective-permute-done((f32[8,128]{1,0:T(8,128)}, f32[8,128]{1,0:T(8,128)S(1)}, u32[]{:S(2)}, u32[]{:S(2)}) %collective-permute-start) | collective-permute-done | bytes 4128 | tf_op jit(solution)/shard_map/ppermute | solution.py:34
  51.9 0.1 reshape.1259
  52.0 10.6 %all-to-all-done.held_out_ref = f32[32,256,128]{2,1,0:T(8,128)} async-done(((f32[32,256,128]{2,1,0:T(8,128)}), f32[32,256,128]{2,1,0:T(8,128)}, u32[]{:S(2)}, u32[]{:S(2)}) %all-to-all-start) | async-done | bytes 4194336 | tf_op jit(solution)/shard_map/all_to_all | solution.py:484
  62.6 9.4 %relax.1 = f32[32,256,128]{2,1,0:T(8,128)} custom-call(s32[768]{0:T(1024)} %get-tuple-element.122.plan_ref, f32[8,128]{1,0:T(8,128)} %get-tuple-element.121.low_ref, f32[8,128]{1,0:T(8,128)} %copy-done.8, f32[8,128]{1,0:T(8,128)} %minimum_divide_fusion.fraction_ref, bf16[144,1024]{1,0:T(8,128)(2,1)} %constant.427.clone.matrix_ref, ...), custom_call_target="tpu_custom_call" | custom-call | tf_op jit(solution)/shard_map/relax/pallas_call | solution.py:372
  72.0 0.0 copy-start.9
  72.1 0.0 copy-start.10
  72.1 0.0 copy-start.11
  72.1 0.0 copy-start.12
  72.1 0.0 copy-start.13
  72.1 5.0 %all-to-all-start.1 = ((f32[32,256,128]{2,1,0:T(8,128)}), f32[32,256,128]{2,1,0:T(8,128)}, u32[]{:S(2)}, u32[]{:S(2)}) async-start(f32[32,256,128]{2,1,0:T(8,128)} %relax.1), calls=%async_computation.1 | async-start | bytes 8388608 | tf_op jit(solution)/shard_map/all_to_all | solution.py:484
  77.2 0.1 slice.585
  77.3 0.1 slice.595
  77.3 0.1 maximum_subtract_fusion.1
  77.4 0.1 slice.593
  77.5 0.1 fusion.61
  77.6 0.1 slice_maximum_fusion.2
  77.7 0.1 fusion.54
  77.8 0.1 stack.18
  77.9 0.1 broadcast_add_fusion
  78.0 0.2 fusion.last_ref
  78.3 2.2 %copy-done = f32[32,256,128]{2,1,0:T(8,128)S(1)} copy-done((f32[32,256,128]{2,1,0:T(8,128)S(1)}, f32[32,256,128]{2,1,0:T(8,128)}, u32[]{:S(2)}) %copy-start) | copy-done | bytes 4194328
  80.4 14.9 %cell_stress.1 = f32[768,128]{1,0:T(8,128)S(1)} custom-call(s32[768]{0:T(1024)S(1)} %copy-done.2, s32[32,128]{1,0:T(8,128)S(1)} %copy-done.1, f32[128,128]{1,0:T(8,128)S(1)} %fusion.last_ref, f32[192,128]{1,0:T(8,128)S(1)} %bitcast_select_fusion.basis_ref, f32[8192,128]{1,0:T(8,128)S(1)} %bitcast.290), custom_call_target="tpu_custom_call" | custom-call | tf_op jit(solution)/shard_map/cell_stress/pallas_call | solution.py:424
  95.3 0.2 reduce_sum.9
  95.6 0.1 reshape.1265
  95.7 0.1 slice.619
  95.8 0.1 slice_maximum_fusion
  95.9 0.1 fusion.44
  96.0 2.0 %collective-permute-start.1 = (f32[3,1,8,16]{3,2,0,1:T(8,128)S(1)}, f32[3,1,8,16]{3,2,0,1:T(8,128)S(1)}, u32[]{:S(2)}, u32[]{:S(2)}) collective-permute-start(f32[3,1,8,16]{3,2,0,1:T(8,128)S(1)} %fusion.44), channel_id=1, source_target_pairs={{0,1},{1,2},{2,3},{3,4},{4,5},{5,6},{6,7},{7,8},{8,9},{9,10},{10,1... | collective-permute-start | bytes 4616 | tf_op jit(solution)/shard_map/ppermute | solution.py:34
  98.0 0.1 slice_maximum_fusion.1
  98.0 0.1 slice.611
  98.1 27.9 %collective-permute-done.1 = f32[3,1,8,16]{3,2,0,1:T(8,128)S(1)} collective-permute-done((f32[3,1,8,16]{3,2,0,1:T(8,128)S(1)}, f32[3,1,8,16]{3,2,0,1:T(8,128)S(1)}, u32[]{:S(2)}, u32[]{:S(2)}) %collective-permute-start.1) | collective-permute-done | bytes 1568 | tf_op jit(solution)/shard_map/ppermute | solution.py:34
  126.0 0.7 fusion.50
  126.7 3.9 %all-to-all-done.1 = f32[32,256,128]{2,1,0:T(8,128)} async-done(((f32[32,256,128]{2,1,0:T(8,128)}), f32[32,256,128]{2,1,0:T(8,128)}, u32[]{:S(2)}, u32[]{:S(2)}) %all-to-all-start.1) | async-done | bytes 4194336 | tf_op jit(solution)/shard_map/all_to_all | solution.py:484
  130.6 3.3 %hand_over.1 = f32[256,4096]{1,0:T(8,128)} custom-call(f32[256,4096]{1,0:T(8,128)} %bitcast.40.received_ref), custom_call_target="tpu_custom_call" | custom-call | tf_op jit(solution)/shard_map/hand_over/pallas_call | solution.py:458
  (57 shorter events, 0.3 us)
Async XLA Ops:
  0.6 8.5 %copy-start.6 = (f32[3,1,8,16]{3,2,1,0:T(8,128)S(1)}, f32[3,1,8,16]{3,2,1,0:T(8,128)}, u32[]{:S(2)}) copy-start(f32[3,1,8,16]{3,2,1,0:T(8,128)} %param.34) | copy-start | bytes 4612
  0.6 8.5 %copy-start.7 = (f32[3,1,8,16]{3,2,1,0:T(8,128)S(1)}, f32[3,1,8,16]{3,2,1,0:T(8,128)}, u32[]{:S(2)}) copy-start(f32[3,1,8,16]{3,2,1,0:T(8,128)} %param.33) | copy-start | bytes 4612
  0.7 22.3 %copy-start.15 = (s32[128]{0:T(128)S(1)}, s32[128]{0:T(128)}, u32[]{:S(2)}) copy-start(s32[128]{0:T(128)} %steps_ref.1) | copy-start | bytes 1540
  0.7 23.0 %copy-start.5 = (s32[2,4096]{1,0:T(2,128)S(1)}, s32[2,4096]{1,0:T(2,128)}, u32[]{:S(2)}) copy-start(s32[2,4096]{1,0:T(2,128)} %param.38) | copy-start | bytes 98308
  0.7 24.5 %copy-start.3 = (f32[6,128]{0,1:T(8,128)S(1)}, f32[6,128]{0,1:T(8,128)}, u32[]{:S(2)}) copy-start(f32[6,128]{0,1:T(8,128)} %constant.429.clone) | copy-start | bytes 9220
  0.7 61.9 %all-to-all-start = ((f32[32,256,128]{2,1,0:T(8,128)}), f32[32,256,128]{2,1,0:T(8,128)}, u32[]{:S(2)}, u32[]{:S(2)}) async-start(f32[32,256,128]{2,1,0:T(8,128)} %bitcast.291), calls=%async_computation | async-start | bytes 8388608 | tf_op jit(solution)/shard_map/all_to_all | solution.py:484
  9.2 68.0 %copy-start.4 = (f32[3,1,8,16]{3,2,1,0:T(8,128)}, f32[3,1,8,16]{3,2,1,0:T(8,128)S(1)}, u32[]{:S(2)}) copy-start(f32[3,1,8,16]{3,2,1,0:T(8,128)S(1)} %multiply_add_fusion.5) | copy-start | bytes 4612
  15.9 36.0 %collective-permute-start = (f32[8,128]{1,0:T(8,128)}, f32[8,128]{1,0:T(8,128)S(1)}, u32[]{:S(2)}, u32[]{:S(2)}) collective-permute-start(f32[8,128]{1,0:T(8,128)} %get-tuple-element.121.low_ref), channel_id=1, source_target_pairs={{1,0},{2,1},{3,2},{4,3},{5,4},{6,5},{7,6},{8,7},{9,8},{10,9},{11,1... | collective-permute-start | bytes 12296 | tf_op jit(solution)/shard_map/ppermute | solution.py:34
  51.9 10.7 %copy-start.8 = (f32[8,128]{1,0:T(8,128)}, f32[8,128]{1,0:T(8,128)S(1)}, u32[]{:S(2)}) copy-start(f32[8,128]{1,0:T(8,128)S(1)} %collective-permute-done.high_ref) | copy-start | bytes 12292
  72.0 5.9 %copy-start.9 = (f32[128]{0:T(128)S(1)}, f32[128]{0:T(128)}, u32[]{:S(2)}) copy-start(f32[128]{0:T(128)} %constant.437) | copy-start | bytes 1540
  72.1 5.9 %copy-start.10 = (f32[128]{0:T(128)S(1)}, f32[128]{0:T(128)}, u32[]{:S(2)}) copy-start(f32[128]{0:T(128)} %constant.439) | copy-start | bytes 1540
  72.1 5.9 %copy-start.11 = (f32[128]{0:T(128)S(1)}, f32[128]{0:T(128)}, u32[]{:S(2)}) copy-start(f32[128]{0:T(128)} %constant.441) | copy-start | bytes 1540
  72.1 5.9 %copy-start.12 = (f32[128]{0:T(128)S(1)}, f32[128]{0:T(128)}, u32[]{:S(2)}) copy-start(f32[128]{0:T(128)} %constant.443) | copy-start | bytes 1540
  72.1 5.9 %copy-start.13 = (f32[128]{0:T(128)S(1)}, f32[128]{0:T(128)}, u32[]{:S(2)}) copy-start(f32[128]{0:T(128)} %constant.445) | copy-start | bytes 1540
  72.1 5.9 %copy-start.14 = (f32[128]{0:T(128)S(1)}, f32[128]{0:T(128)}, u32[]{:S(2)}) copy-start(f32[128]{0:T(128)} %constant.447) | copy-start | bytes 1540
  72.1 6.1 %copy-start.1 = (s32[32,128]{1,0:T(8,128)S(1)}, s32[32,128]{1,0:T(8,128)}, u32[]{:S(2)}) copy-start(s32[32,128]{1,0:T(8,128)} %get-tuple-element.124.codes_ref) | copy-start | bytes 49156
  72.1 6.1 %copy-start.2 = (s32[768]{0:T(1024)S(1)}, s32[768]{0:T(1024)}, u32[]{:S(2)}) copy-start(s32[768]{0:T(1024)} %get-tuple-element.122.plan_ref) | copy-start | bytes 9220
  72.1 58.5 %all-to-all-start.1 = ((f32[32,256,128]{2,1,0:T(8,128)}), f32[32,256,128]{2,1,0:T(8,128)}, u32[]{:S(2)}, u32[]{:S(2)}) async-start(f32[32,256,128]{2,1,0:T(8,128)} %relax.1), calls=%async_computation.1 | async-start | bytes 8388608 | tf_op jit(solution)/shard_map/all_to_all | solution.py:484
  78.2 2.2 %copy-start = (f32[32,256,128]{2,1,0:T(8,128)S(1)}, f32[32,256,128]{2,1,0:T(8,128)}, u32[]{:S(2)}) copy-start(f32[32,256,128]{2,1,0:T(8,128)} %relax.1) | copy-start | bytes 12582916
  96.0 30.0 %collective-permute-start.1 = (f32[3,1,8,16]{3,2,0,1:T(8,128)S(1)}, f32[3,1,8,16]{3,2,0,1:T(8,128)S(1)}, u32[]{:S(2)}, u32[]{:S(2)}) collective-permute-start(f32[3,1,8,16]{3,2,0,1:T(8,128)S(1)} %fusion.44), channel_id=1, source_target_pairs={{0,1},{1,2},{2,3},{3,4},{4,5},{5,6},{6,7},{7,8},{8,9},{9,10},{10,1... | collective-permute-start | bytes 4616 | tf_op jit(solution)/shard_map/ppermute | solution.py:34
